TPU v7x, 32 devices: a whole 2x2x4 slice. The times are simulated.
32 devices in a mesh: gx: 4 (over z), gy: 2 (over core), gz: 4 (over y, x).
Axes of the slice: x: 2, y: 2, z: 4, core: 2. Of those that a mesh axis runs over, the one named last changes fastest.
Arguments:
- traces: bfloat16 [2048, 32], P('gx'), may hold values from -6 to 6
- receiver_cell: int32 [2048], P('gx'), may hold values from 0 to 2047
- weight_class: int32 [2048], P('gx'), may hold values from 0 to 15
- weight_table: float32 [16], replicated, may hold values from 0.5 to 2
- obstacle_top: int32 [8, 64], P('gx', 'gy'), may hold values from 128 to 255
- obstacle_thick: int32 [8, 64], P('gx', 'gy'), may hold values from 0 to 128
- courant: float32 [16, 128, 512], P('gx', 'gy', 'gz'), may hold values from 0.06 to 0.25
- p_now: float32 [16, 128, 512], P('gx', 'gy', 'gz'), may hold values from -6 to 6
- p_prev: float32 [16, 128, 512], P('gx', 'gy', 'gz'), may hold values from -6 to 6
Outputs:
- wavefield: float32 [16, 128, 512], P('gx', 'gy', 'gz')
All inputs are finite; a program needn't handle non-finite values.
Results may differ from a plain program's by a relative error of at most 0.0003.
Values may be sent and summed in bfloat16 or wider, within the bound.
A program may use at most 64 MiB of HBM per device.

v0:
```python
import jax
import jax.numpy as jnp
from jax import lax
from jax.sharding import PartitionSpec as P


def with_halo(cells, sides, width):
    for axis, dim in sides:
        count = lax.axis_size(axis)
        ends = count - 1
        head = lax.slice_in_dim(cells, 0, width, axis=dim)
        tail = lax.slice_in_dim(cells, cells.shape[dim] - width, cells.shape[dim], axis=dim)
        cells = jnp.concatenate(
            [
                lax.ppermute(tail, axis, [(i, (i + 1) % count) for i in range(ends)]),
                cells,
                lax.ppermute(head, axis, [((i + 1) % count, i) for i in range(ends)]),
            ],
            axis=dim,
        )
    return cells


def receiver_terms(trace_rows, class_rows, weight_table):
    one_hot = (
        class_rows[:, None] == jnp.arange(weight_table.shape[0], dtype=jnp.int32)[None, :]
    ).astype(jnp.float32)
    weights = jnp.sum(one_hot * weight_table[None, :], axis=1)
    return weights[:, None] * trace_rows.astype(jnp.float32)


def advance(wavefield, before, speeds, living, source_plane, depth_select):
    centre = wavefield[1:-1, 1:-1, 1:-1]
    beside_all = wavefield[2:, 1:-1, 1:-1] + wavefield[:-2, 1:-1, 1:-1]
    beside_all = beside_all + wavefield[1:-1, 2:, 1:-1] + wavefield[1:-1, :-2, 1:-1]
    beside_all = beside_all + wavefield[1:-1, 1:-1, 2:] + wavefield[1:-1, 1:-1, :-2]
    laplace = beside_all - 6.0 * centre
    updated = 2.0 * centre - before + speeds * laplace + source_plane[:, :, None] * depth_select
    return living * updated


def local(
    traces,
    receiver_cell,
    weight_class,
    weight_table,
    obstacle_top,
    obstacle_thick,
    courant,
    p_now,
    p_prev,
):
    tile_x, tile_y, tile_z = courant.shape
    step_count = traces.shape[1]
    grid_y = tile_y * lax.axis_size("gy")
    anchor_x = lax.axis_index("gx") * tile_x
    anchor_y = lax.axis_index("gy") * tile_y
    anchor_z = lax.axis_index("gz") * tile_z
    roof = jnp.repeat(jnp.repeat(obstacle_top, 2, axis=0), 2, axis=1)[:, :, None]
    thickness = jnp.repeat(jnp.repeat(obstacle_thick, 2, axis=0), 2, axis=1)[:, :, None]
    depth_cells = anchor_z + jnp.arange(tile_z, dtype=jnp.int32)[None, None, :]
    solid = (depth_cells >= roof) & (depth_cells < roof + thickness)
    living = jnp.where(solid, 0.0, 1.0).astype(jnp.float32)
    trace_rows = lax.all_gather(traces, "gx", axis=0, tiled=True)
    cell_rows = lax.all_gather(receiver_cell, "gx", axis=0, tiled=True)
    class_rows = lax.all_gather(weight_class, "gx", axis=0, tiled=True)
    contrib = receiver_terms(trace_rows, class_rows, weight_table)
    cell_x = cell_rows // grid_y
    cell_y = cell_rows % grid_y
    inside = (
        (cell_x >= anchor_x)
        & (cell_x < anchor_x + tile_x)
        & (cell_y >= anchor_y)
        & (cell_y < anchor_y + tile_y)
    )
    segment = jnp.where(inside, (cell_x - anchor_x) * tile_y + cell_y - anchor_y, tile_x * tile_y)
    accumulated = jax.ops.segment_sum(contrib, segment, num_segments=tile_x * tile_y + 1)
    sources = accumulated[:-1].reshape(tile_x, tile_y, step_count)
    surface_flag = (anchor_z == 0).astype(jnp.float32)
    sources = sources * surface_flag
    depth_first = (jnp.arange(tile_z, dtype=jnp.int32) == 0).astype(jnp.float32)
    statics = with_halo(jnp.stack([courant, living]), (("gx", 1), ("gy", 2), ("gz", 3)), 2)
    source_ext = with_halo(sources, (("gx", 0), ("gy", 1)), 2)
    speeds_mid = statics[0, 1:-1, 1:-1, 1:-1]
    living_mid = statics[1, 1:-1, 1:-1, 1:-1]
    depth_second = (jnp.arange(tile_z + 2, dtype=jnp.int32) == 1).astype(jnp.float32)

    def double_step(counter, carried):
        current, previous = carried
        stacked = with_halo(jnp.stack([current, previous]), (("gx", 1), ("gy", 2), ("gz", 3)), 2)
        present = stacked[0]
        earlier = stacked[1]
        first_step = 2 * counter
        plane_one = lax.dynamic_index_in_dim(
            source_ext, step_count - 1 - first_step, 2, keepdims=False
        )[1:-1, 1:-1]
        halfway = advance(
            present, earlier[1:-1, 1:-1, 1:-1], speeds_mid, living_mid, plane_one, depth_second
        )
        plane_two = lax.dynamic_index_in_dim(
            source_ext, step_count - 2 - first_step, 2, keepdims=False
        )[2:-2, 2:-2]
        updated = advance(
            halfway, present[2:-2, 2:-2, 2:-2], courant, living, plane_two, depth_first
        )
        return (updated, halfway[1:-1, 1:-1, 1:-1])

    current, previous = lax.fori_loop(0, step_count // 2, double_step, (p_now, p_prev))
    return current


def solution(mesh):
    placed = (
        P("gx", None),
        P("gx"),
        P("gx"),
        P(),
        P("gx", "gy"),
        P("gx", "gy"),
        P("gx", "gy", "gz"),
        P("gx", "gy", "gz"),
        P("gx", "gy", "gz"),
    )
    return jax.shard_map(
        local, mesh=mesh, in_specs=placed, out_specs=P("gx", "gy", "gz"), check_vma=False
    )
```

profile of v0, /device:TPU:0, one launch (start us, length us, event | category | flops | bytes accessed | tf_op | source)
XLA Modules:
  0.0 524.2 jit_solution(12124108732362166365)
XLA Ops:
  0.0 13.7 %all-gather = s32[4,1,512]{2,1,0:T(1,128)S(1)} all-gather(s32[1,1,512]{2,1,0:T(1,128)} %bitcast.58), channel_id=1, replica_groups=mesh['gx'=4,'gy'=2,'gz'=4] {'gx'}, dimensions={0}, use_global_device_ids=true | all-gather | bytes 10240 | tf_op jit(solution)/shard_map/all_gather | solution.py:65
  13.7 13.5 %all_gather.11 = bf16[2048,32]{0,1:T(8,128)(2,1)S(1)} all-gather(bf16[512,32]{0,1:T(8,128)(2,1)} %param.11), channel_id=1, replica_groups=mesh['gx'=4,'gy'=2,'gz'=4] {'gx'}, dimensions={0}, use_global_device_ids=true | all-gather | bytes 163840 | tf_op jit(solution)/shard_map/all_gather | solution.py:64
  27.2 12.0 %all-gather.1 = s32[4,1,512]{2,1,0:T(1,128)S(1)} all-gather(s32[1,1,512]{2,1,0:T(1,128)} %bitcast.59), channel_id=1, replica_groups=mesh['gx'=4,'gy'=2,'gz'=4] {'gx'}, dimensions={0}, use_global_device_ids=true | all-gather | bytes 10240 | tf_op jit(solution)/shard_map/all_gather | solution.py:66
  40.4 12.9 %scatter_custom_fusion = f32[257,32]{1,0:T(8,128)S(1)} fusion(s32[2048]{0:T(1024)S(1)} %subtract_select_fusion, f32[2048,32]{1,0:T(8,128)S(1)} %copy.85, f32[]{:T(128)} %constant.132.clone.1), kind=kCustom, calls=%fused_computation.57 | custom fusion | flops 65536 | bytes 32900 | tf_op jit(solution)/shard_map/scatter-add | solution.py:77
  53.4 2.4 collective-permute-start.12
  57.9 4.6 collective-permute-start.6
  64.9 4.4 collective-permute-done.7
  72.0 3.0 collective-permute-start.14
  77.0 3.4 collective-permute-start.10
  83.0 3.4 collective-permute-done.11
  88.1 435.5 %while.18 = (s32[]{:T(128)}, f32[4,64,128]{2,0,1:T(4,128)S(1)}, f32[4,64,128]{2,0,1:T(4,128)S(1)}, f32[6,66,130]{2,0,1:T(8,128)S(1)}, f32[8,68,32]{0,1,2:T(8,128...) while((s32[]{:T(128)}, f32[4,64,128]{2,0,1:T(4,128)S(1)}, ...), condition=%wide.region_3.4_spmd.clone, body=%wide.region_2.3_spmd.clone.sunk | while | flops 3102815 | bytes 10132725 | solution.py:108
  89.5 4.6 collective-permute-start.1
  94.1 1.4 collective-permute-done
  98.0 3.0 collective-permute-start.3
  102.5 1.3 collective-permute-start.4
  104.1 4.9 collective-permute-start.5
  115.7 5.0 collective-permute-start.1
  124.6 3.0 collective-permute-start.3
  130.6 5.4 %collective-permute-start.5 = (f32[2,8,68,2]{2,1,3,0:T(8,128)S(1)}, f32[2,8,68,2]{2,1,3,0:T(8,128)S(1)}, u32[]{:S(2)}, u32[]{:S(2)}) collective-permute-start(f32[2,8,68,2]{2,1,3,0:T(8,128)S(1)} %copy.103), channel_id=1, source_target_pairs={{0,1},{1,2},{2,3},{4,5},{5,6},{6,7},{8,9},{9,10},{10,11},{12,13},{... | collective-permute-start | bytes 26120 | tf_op jit(solution)/shard_map/while/body/eval_jaxpr/ppermute | solution.py:15
  142.8 5.0 collective-permute-start.1
  151.6 3.0 collective-permute-start.3
  156.1 1.3 collective-permute-start.4
  157.7 5.7 %collective-permute-start.5 = (f32[2,8,68,2]{2,1,3,0:T(8,128)S(1)}, f32[2,8,68,2]{2,1,3,0:T(8,128)S(1)}, u32[]{:S(2)}, u32[]{:S(2)}) collective-permute-start(f32[2,8,68,2]{2,1,3,0:T(8,128)S(1)} %copy.103), channel_id=1, source_target_pairs={{0,1},{1,2},{2,3},{4,5},{5,6},{6,7},{8,9},{9,10},{10,11},{12,13},{... | collective-permute-start | bytes 26120 | tf_op jit(solution)/shard_map/while/body/eval_jaxpr/ppermute | solution.py:15
  170.1 5.0 collective-permute-start.1
  178.9 3.0 collective-permute-start.3
  183.4 1.3 collective-permute-start.4
  185.0 5.7 %collective-permute-start.5 = (f32[2,8,68,2]{2,1,3,0:T(8,128)S(1)}, f32[2,8,68,2]{2,1,3,0:T(8,128)S(1)}, u32[]{:S(2)}, u32[]{:S(2)}) collective-permute-start(f32[2,8,68,2]{2,1,3,0:T(8,128)S(1)} %copy.103), channel_id=1, source_target_pairs={{0,1},{1,2},{2,3},{4,5},{5,6},{6,7},{8,9},{9,10},{10,11},{12,13},{... | collective-permute-start | bytes 26120 | tf_op jit(solution)/shard_map/while/body/eval_jaxpr/ppermute | solution.py:15
  197.4 5.0 collective-permute-start.1
  206.2 3.0 collective-permute-start.3
  212.3 5.7 %collective-permute-start.5 = (f32[2,8,68,2]{2,1,3,0:T(8,128)S(1)}, f32[2,8,68,2]{2,1,3,0:T(8,128)S(1)}, u32[]{:S(2)}, u32[]{:S(2)}) collective-permute-start(f32[2,8,68,2]{2,1,3,0:T(8,128)S(1)} %copy.103), channel_id=1, source_target_pairs={{0,1},{1,2},{2,3},{4,5},{5,6},{6,7},{8,9},{9,10},{10,11},{12,13},{... | collective-permute-start | bytes 26120 | tf_op jit(solution)/shard_map/while/body/eval_jaxpr/ppermute | solution.py:15
  224.7 5.0 collective-permute-start.1
  233.5 3.0 collective-permute-start.3
  238.0 1.3 collective-permute-start.4
  239.6 5.7 %collective-permute-start.5 = (f32[2,8,68,2]{2,1,3,0:T(8,128)S(1)}, f32[2,8,68,2]{2,1,3,0:T(8,128)S(1)}, u32[]{:S(2)}, u32[]{:S(2)}) collective-permute-start(f32[2,8,68,2]{2,1,3,0:T(8,128)S(1)} %copy.103), channel_id=1, source_target_pairs={{0,1},{1,2},{2,3},{4,5},{5,6},{6,7},{8,9},{9,10},{10,11},{12,13},{... | collective-permute-start | bytes 26120 | tf_op jit(solution)/shard_map/while/body/eval_jaxpr/ppermute | solution.py:15
  252.0 5.0 collective-permute-start.1
  260.8 3.0 collective-permute-start.3
  266.9 5.7 %collective-permute-start.5 = (f32[2,8,68,2]{2,1,3,0:T(8,128)S(1)}, f32[2,8,68,2]{2,1,3,0:T(8,128)S(1)}, u32[]{:S(2)}, u32[]{:S(2)}) collective-permute-start(f32[2,8,68,2]{2,1,3,0:T(8,128)S(1)} %copy.103), channel_id=1, source_target_pairs={{0,1},{1,2},{2,3},{4,5},{5,6},{6,7},{8,9},{9,10},{10,11},{12,13},{... | collective-permute-start | bytes 26120 | tf_op jit(solution)/shard_map/while/body/eval_jaxpr/ppermute | solution.py:15
  279.3 5.0 collective-permute-start.1
  288.1 3.0 collective-permute-start.3
  294.2 5.7 %collective-permute-start.5 = (f32[2,8,68,2]{2,1,3,0:T(8,128)S(1)}, f32[2,8,68,2]{2,1,3,0:T(8,128)S(1)}, u32[]{:S(2)}, u32[]{:S(2)}) collective-permute-start(f32[2,8,68,2]{2,1,3,0:T(8,128)S(1)} %copy.103), channel_id=1, source_target_pairs={{0,1},{1,2},{2,3},{4,5},{5,6},{6,7},{8,9},{9,10},{10,11},{12,13},{... | collective-permute-start | bytes 26120 | tf_op jit(solution)/shard_map/while/body/eval_jaxpr/ppermute | solution.py:15
  306.6 5.0 collective-permute-start.1
  315.4 3.0 collective-permute-start.3
  321.5 5.7 %collective-permute-start.5 = (f32[2,8,68,2]{2,1,3,0:T(8,128)S(1)}, f32[2,8,68,2]{2,1,3,0:T(8,128)S(1)}, u32[]{:S(2)}, u32[]{:S(2)}) collective-permute-start(f32[2,8,68,2]{2,1,3,0:T(8,128)S(1)} %copy.103), channel_id=1, source_target_pairs={{0,1},{1,2},{2,3},{4,5},{5,6},{6,7},{8,9},{9,10},{10,11},{12,13},{... | collective-permute-start | bytes 26120 | tf_op jit(solution)/shard_map/while/body/eval_jaxpr/ppermute | solution.py:15
  333.9 5.0 collective-permute-start.1
  342.7 3.0 collective-permute-start.3
  348.8 5.7 %collective-permute-start.5 = (f32[2,8,68,2]{2,1,3,0:T(8,128)S(1)}, f32[2,8,68,2]{2,1,3,0:T(8,128)S(1)}, u32[]{:S(2)}, u32[]{:S(2)}) collective-permute-start(f32[2,8,68,2]{2,1,3,0:T(8,128)S(1)} %copy.103), channel_id=1, source_target_pairs={{0,1},{1,2},{2,3},{4,5},{5,6},{6,7},{8,9},{9,10},{10,11},{12,13},{... | collective-permute-start | bytes 26120 | tf_op jit(solution)/shard_map/while/body/eval_jaxpr/ppermute | solution.py:15
  361.2 5.0 collective-permute-start.1
  370.0 3.0 collective-permute-start.3
  376.1 5.7 %collective-permute-start.5 = (f32[2,8,68,2]{2,1,3,0:T(8,128)S(1)}, f32[2,8,68,2]{2,1,3,0:T(8,128)S(1)}, u32[]{:S(2)}, u32[]{:S(2)}) collective-permute-start(f32[2,8,68,2]{2,1,3,0:T(8,128)S(1)} %copy.103), channel_id=1, source_target_pairs={{0,1},{1,2},{2,3},{4,5},{5,6},{6,7},{8,9},{9,10},{10,11},{12,13},{... | collective-permute-start | bytes 26120 | tf_op jit(solution)/shard_map/while/body/eval_jaxpr/ppermute | solution.py:15
  388.5 5.0 collective-permute-start.1
  397.3 3.0 collective-permute-start.3
  403.4 5.7 %collective-permute-start.5 = (f32[2,8,68,2]{2,1,3,0:T(8,128)S(1)}, f32[2,8,68,2]{2,1,3,0:T(8,128)S(1)}, u32[]{:S(2)}, u32[]{:S(2)}) collective-permute-start(f32[2,8,68,2]{2,1,3,0:T(8,128)S(1)} %copy.103), channel_id=1, source_target_pairs={{0,1},{1,2},{2,3},{4,5},{5,6},{6,7},{8,9},{9,10},{10,11},{12,13},{... | collective-permute-start | bytes 26120 | tf_op jit(solution)/shard_map/while/body/eval_jaxpr/ppermute | solution.py:15
  415.8 5.0 collective-permute-start.1
  424.6 3.0 collective-permute-start.3
  430.7 5.7 %collective-permute-start.5 = (f32[2,8,68,2]{2,1,3,0:T(8,128)S(1)}, f32[2,8,68,2]{2,1,3,0:T(8,128)S(1)}, u32[]{:S(2)}, u32[]{:S(2)}) collective-permute-start(f32[2,8,68,2]{2,1,3,0:T(8,128)S(1)} %copy.103), channel_id=1, source_target_pairs={{0,1},{1,2},{2,3},{4,5},{5,6},{6,7},{8,9},{9,10},{10,11},{12,13},{... | collective-permute-start | bytes 26120 | tf_op jit(solution)/shard_map/while/body/eval_jaxpr/ppermute | solution.py:15
  443.1 5.0 collective-permute-start.1
  451.9 3.0 collective-permute-start.3
  458.0 5.7 %collective-permute-start.5 = (f32[2,8,68,2]{2,1,3,0:T(8,128)S(1)}, f32[2,8,68,2]{2,1,3,0:T(8,128)S(1)}, u32[]{:S(2)}, u32[]{:S(2)}) collective-permute-start(f32[2,8,68,2]{2,1,3,0:T(8,128)S(1)} %copy.103), channel_id=1, source_target_pairs={{0,1},{1,2},{2,3},{4,5},{5,6},{6,7},{8,9},{9,10},{10,11},{12,13},{... | collective-permute-start | bytes 26120 | tf_op jit(solution)/shard_map/while/body/eval_jaxpr/ppermute | solution.py:15
  470.4 5.0 collective-permute-start.1
  479.2 3.0 collective-permute-start.3
  485.3 5.7 %collective-permute-start.5 = (f32[2,8,68,2]{2,1,3,0:T(8,128)S(1)}, f32[2,8,68,2]{2,1,3,0:T(8,128)S(1)}, u32[]{:S(2)}, u32[]{:S(2)}) collective-permute-start(f32[2,8,68,2]{2,1,3,0:T(8,128)S(1)} %copy.103), channel_id=1, source_target_pairs={{0,1},{1,2},{2,3},{4,5},{5,6},{6,7},{8,9},{9,10},{10,11},{12,13},{... | collective-permute-start | bytes 26120 | tf_op jit(solution)/shard_map/while/body/eval_jaxpr/ppermute | solution.py:15
  497.7 5.0 collective-permute-start.1
  506.5 3.0 collective-permute-start.3
  512.6 5.7 %collective-permute-start.5 = (f32[2,8,68,2]{2,1,3,0:T(8,128)S(1)}, f32[2,8,68,2]{2,1,3,0:T(8,128)S(1)}, u32[]{:S(2)}, u32[]{:S(2)}) collective-permute-start(f32[2,8,68,2]{2,1,3,0:T(8,128)S(1)} %copy.103), channel_id=1, source_target_pairs={{0,1},{1,2},{2,3},{4,5},{5,6},{6,7},{8,9},{9,10},{10,11},{12,13},{... | collective-permute-start | bytes 26120 | tf_op jit(solution)/shard_map/while/body/eval_jaxpr/ppermute | solution.py:15
  (535 shorter events, 223.3 us)
Async XLA Ops:
  53.4 10.6 %collective-permute-start.12 = (f32[2,64,32]{1,2,0:T(8,128)S(1)}, f32[2,64,32]{1,2,0:T(8,128)S(1)}, u32[]{:S(2)}, u32[]{:S(2)}) collective-permute-start(f32[2,64,32]{1,2,0:T(8,128)S(1)} %copy.86), channel_id=1, source_target_pairs={{0,8},{8,16},{16,24},{1,9},{9,17},{17,25},{2,10},{10,18},{18,26},{... | collective-permute-start | bytes 49160 | tf_op jit(solution)/shard_map/ppermute | solution.py:15
  55.9 8.2 %collective-permute-start.13 = (f32[2,64,32]{1,2,0:T(8,128)S(1)}, f32[2,64,32]{1,2,0:T(8,128)S(1)}, u32[]{:S(2)}, u32[]{:S(2)}) collective-permute-start(f32[2,64,32]{1,2,0:T(8,128)S(1)} %copy.87), channel_id=1, source_target_pairs={{8,0},{16,8},{24,16},{9,1},{17,9},{25,17},{10,2},{18,10},{26,18},{... | collective-permute-start | bytes 49160 | tf_op jit(solution)/shard_map/ppermute | solution.py:17
  72.0 10.0 %collective-permute-start.14 = (f32[8,2,32]{1,2,0:T(8,128)S(1)}, f32[8,2,32]{1,2,0:T(8,128)S(1)}, u32[]{:S(2)}, u32[]{:S(2)}) collective-permute-start(f32[8,2,32]{1,2,0:T(8,128)S(1)} %get-tuple-element.368), channel_id=1, source_target_pairs={{0,4},{1,5},{2,6},{3,7},{8,12},{9,13},{10,14},{11,15},{16,20},{17,... | collective-permute-start | bytes 6152 | tf_op jit(solution)/shard_map/ppermute | solution.py:15
  88.2 7.3 %collective-permute-start = (f32[2,2,64,128]{3,1,2,0:T(2,128)S(1)}, f32[2,2,64,128]{3,1,2,0:T(2,128)S(1)}, u32[]{:S(2)}, u32[]{:S(2)}) collective-permute-start(f32[2,2,64,128]{3,1,2,0:T(2,128)S(1)} %get-tuple-element.445), channel_id=1, source_target_pairs={{8,0},{16,8},{24,16},{9,1},{17,9},{25,17},{10,2},{18,10},{26,18},{... | collective-permute-start | bytes 393224 | tf_op jit(solution)/shard_map/while/body/eval_jaxpr/ppermute | solution.py:17
  89.5 7.2 %collective-permute-start.1 = (f32[2,2,64,128]{3,1,2,0:T(2,128)S(1)}, f32[2,2,64,128]{3,1,2,0:T(2,128)S(1)}, u32[]{:S(2)}, u32[]{:S(2)}) collective-permute-start(f32[2,2,64,128]{3,1,2,0:T(2,128)S(1)} %get-tuple-element.446), channel_id=1, source_target_pairs={{0,8},{8,16},{16,24},{1,9},{9,17},{17,25},{2,10},{10,18},{18,26},{... | collective-permute-start | bytes 393224 | tf_op jit(solution)/shard_map/while/body/eval_jaxpr/ppermute | solution.py:15
  114.4 7.5 %collective-permute-start = (f32[2,2,64,128]{3,1,2,0:T(2,128)S(1)}, f32[2,2,64,128]{3,1,2,0:T(2,128)S(1)}, u32[]{:S(2)}, u32[]{:S(2)}) collective-permute-start(f32[2,2,64,128]{3,1,2,0:T(2,128)S(1)} %get-tuple-element.445), channel_id=1, source_target_pairs={{8,0},{16,8},{24,16},{9,1},{17,9},{25,17},{10,2},{18,10},{26,18},{... | collective-permute-start | bytes 393224 | tf_op jit(solution)/shard_map/while/body/eval_jaxpr/ppermute | solution.py:17
  115.7 7.5 %collective-permute-start.1 = (f32[2,2,64,128]{3,1,2,0:T(2,128)S(1)}, f32[2,2,64,128]{3,1,2,0:T(2,128)S(1)}, u32[]{:S(2)}, u32[]{:S(2)}) collective-permute-start(f32[2,2,64,128]{3,1,2,0:T(2,128)S(1)} %get-tuple-element.446), channel_id=1, source_target_pairs={{0,8},{8,16},{16,24},{1,9},{9,17},{17,25},{2,10},{10,18},{18,26},{... | collective-permute-start | bytes 393224 | tf_op jit(solution)/shard_map/while/body/eval_jaxpr/ppermute | solution.py:15
  129.1 7.2 %collective-permute-start.4 = (f32[2,8,68,2]{2,1,3,0:T(8,128)S(1)}, f32[2,8,68,2]{2,1,3,0:T(8,128)S(1)}, u32[]{:S(2)}, u32[]{:S(2)}) collective-permute-start(f32[2,8,68,2]{2,1,3,0:T(8,128)S(1)} %copy.101), channel_id=1, source_target_pairs={{1,0},{2,1},{3,2},{5,4},{6,5},{7,6},{9,8},{10,9},{11,10},{13,12},{... | collective-permute-start | bytes 26120 | tf_op jit(solution)/shard_map/while/body/eval_jaxpr/ppermute | solution.py:17
  141.5 7.5 %collective-permute-start = (f32[2,2,64,128]{3,1,2,0:T(2,128)S(1)}, f32[2,2,64,128]{3,1,2,0:T(2,128)S(1)}, u32[]{:S(2)}, u32[]{:S(2)}) collective-permute-start(f32[2,2,64,128]{3,1,2,0:T(2,128)S(1)} %get-tuple-element.445), channel_id=1, source_target_pairs={{8,0},{16,8},{24,16},{9,1},{17,9},{25,17},{10,2},{18,10},{26,18},{... | collective-permute-start | bytes 393224 | tf_op jit(solution)/shard_map/while/body/eval_jaxpr/ppermute | solution.py:17
  142.8 7.5 %collective-permute-start.1 = (f32[2,2,64,128]{3,1,2,0:T(2,128)S(1)}, f32[2,2,64,128]{3,1,2,0:T(2,128)S(1)}, u32[]{:S(2)}, u32[]{:S(2)}) collective-permute-start(f32[2,2,64,128]{3,1,2,0:T(2,128)S(1)} %get-tuple-element.446), channel_id=1, source_target_pairs={{0,8},{8,16},{16,24},{1,9},{9,17},{17,25},{2,10},{10,18},{18,26},{... | collective-permute-start | bytes 393224 | tf_op jit(solution)/shard_map/while/body/eval_jaxpr/ppermute | solution.py:15
  156.1 7.5 %collective-permute-start.4 = (f32[2,8,68,2]{2,1,3,0:T(8,128)S(1)}, f32[2,8,68,2]{2,1,3,0:T(8,128)S(1)}, u32[]{:S(2)}, u32[]{:S(2)}) collective-permute-start(f32[2,8,68,2]{2,1,3,0:T(8,128)S(1)} %copy.101), channel_id=1, source_target_pairs={{1,0},{2,1},{3,2},{5,4},{6,5},{7,6},{9,8},{10,9},{11,10},{13,12},{... | collective-permute-start | bytes 26120 | tf_op jit(solution)/shard_map/while/body/eval_jaxpr/ppermute | solution.py:17
  157.7 7.2 %collective-permute-start.5 = (f32[2,8,68,2]{2,1,3,0:T(8,128)S(1)}, f32[2,8,68,2]{2,1,3,0:T(8,128)S(1)}, u32[]{:S(2)}, u32[]{:S(2)}) collective-permute-start(f32[2,8,68,2]{2,1,3,0:T(8,128)S(1)} %copy.103), channel_id=1, source_target_pairs={{0,1},{1,2},{2,3},{4,5},{5,6},{6,7},{8,9},{9,10},{10,11},{12,13},{... | collective-permute-start | bytes 26120 | tf_op jit(solution)/shard_map/while/body/eval_jaxpr/ppermute | solution.py:15
  168.8 7.5 %collective-permute-start = (f32[2,2,64,128]{3,1,2,0:T(2,128)S(1)}, f32[2,2,64,128]{3,1,2,0:T(2,128)S(1)}, u32[]{:S(2)}, u32[]{:S(2)}) collective-permute-start(f32[2,2,64,128]{3,1,2,0:T(2,128)S(1)} %get-tuple-element.445), channel_id=1, source_target_pairs={{8,0},{16,8},{24,16},{9,1},{17,9},{25,17},{10,2},{18,10},{26,18},{... | collective-permute-start | bytes 393224 | tf_op jit(solution)/shard_map/while/body/eval_jaxpr/ppermute | solution.py:17
  170.1 7.5 %collective-permute-start.1 = (f32[2,2,64,128]{3,1,2,0:T(2,128)S(1)}, f32[2,2,64,128]{3,1,2,0:T(2,128)S(1)}, u32[]{:S(2)}, u32[]{:S(2)}) collective-permute-start(f32[2,2,64,128]{3,1,2,0:T(2,128)S(1)} %get-tuple-element.446), channel_id=1, source_target_pairs={{0,8},{8,16},{16,24},{1,9},{9,17},{17,25},{2,10},{10,18},{18,26},{... | collective-permute-start | bytes 393224 | tf_op jit(solution)/shard_map/while/body/eval_jaxpr/ppermute | solution.py:15
  183.4 7.5 %collective-permute-start.4 = (f32[2,8,68,2]{2,1,3,0:T(8,128)S(1)}, f32[2,8,68,2]{2,1,3,0:T(8,128)S(1)}, u32[]{:S(2)}, u32[]{:S(2)}) collective-permute-start(f32[2,8,68,2]{2,1,3,0:T(8,128)S(1)} %copy.101), channel_id=1, source_target_pairs={{1,0},{2,1},{3,2},{5,4},{6,5},{7,6},{9,8},{10,9},{11,10},{13,12},{... | collective-permute-start | bytes 26120 | tf_op jit(solution)/shard_map/while/body/eval_jaxpr/ppermute | solution.py:17
  185.0 7.2 %collective-permute-start.5 = (f32[2,8,68,2]{2,1,3,0:T(8,128)S(1)}, f32[2,8,68,2]{2,1,3,0:T(8,128)S(1)}, u32[]{:S(2)}, u32[]{:S(2)}) collective-permute-start(f32[2,8,68,2]{2,1,3,0:T(8,128)S(1)} %copy.103), channel_id=1, source_target_pairs={{0,1},{1,2},{2,3},{4,5},{5,6},{6,7},{8,9},{9,10},{10,11},{12,13},{... | collective-permute-start | bytes 26120 | tf_op jit(solution)/shard_map/while/body/eval_jaxpr/ppermute | solution.py:15
  196.1 7.5 %collective-permute-start = (f32[2,2,64,128]{3,1,2,0:T(2,128)S(1)}, f32[2,2,64,128]{3,1,2,0:T(2,128)S(1)}, u32[]{:S(2)}, u32[]{:S(2)}) collective-permute-start(f32[2,2,64,128]{3,1,2,0:T(2,128)S(1)} %get-tuple-element.445), channel_id=1, source_target_pairs={{8,0},{16,8},{24,16},{9,1},{17,9},{25,17},{10,2},{18,10},{26,18},{... | collective-permute-start | bytes 393224 | tf_op jit(solution)/shard_map/while/body/eval_jaxpr/ppermute | solution.py:17
  197.4 7.5 %collective-permute-start.1 = (f32[2,2,64,128]{3,1,2,0:T(2,128)S(1)}, f32[2,2,64,128]{3,1,2,0:T(2,128)S(1)}, u32[]{:S(2)}, u32[]{:S(2)}) collective-permute-start(f32[2,2,64,128]{3,1,2,0:T(2,128)S(1)} %get-tuple-element.446), channel_id=1, source_target_pairs={{0,8},{8,16},{16,24},{1,9},{9,17},{17,25},{2,10},{10,18},{18,26},{... | collective-permute-start | bytes 393224 | tf_op jit(solution)/shard_map/while/body/eval_jaxpr/ppermute | solution.py:15
  210.7 7.5 %collective-permute-start.4 = (f32[2,8,68,2]{2,1,3,0:T(8,128)S(1)}, f32[2,8,68,2]{2,1,3,0:T(8,128)S(1)}, u32[]{:S(2)}, u32[]{:S(2)}) collective-permute-start(f32[2,8,68,2]{2,1,3,0:T(8,128)S(1)} %copy.101), channel_id=1, source_target_pairs={{1,0},{2,1},{3,2},{5,4},{6,5},{7,6},{9,8},{10,9},{11,10},{13,12},{... | collective-permute-start | bytes 26120 | tf_op jit(solution)/shard_map/while/body/eval_jaxpr/ppermute | solution.py:17
  212.3 7.2 %collective-permute-start.5 = (f32[2,8,68,2]{2,1,3,0:T(8,128)S(1)}, f32[2,8,68,2]{2,1,3,0:T(8,128)S(1)}, u32[]{:S(2)}, u32[]{:S(2)}) collective-permute-start(f32[2,8,68,2]{2,1,3,0:T(8,128)S(1)} %copy.103), channel_id=1, source_target_pairs={{0,1},{1,2},{2,3},{4,5},{5,6},{6,7},{8,9},{9,10},{10,11},{12,13},{... | collective-permute-start | bytes 26120 | tf_op jit(solution)/shard_map/while/body/eval_jaxpr/ppermute | solution.py:15
  223.4 7.5 %collective-permute-start = (f32[2,2,64,128]{3,1,2,0:T(2,128)S(1)}, f32[2,2,64,128]{3,1,2,0:T(2,128)S(1)}, u32[]{:S(2)}, u32[]{:S(2)}) collective-permute-start(f32[2,2,64,128]{3,1,2,0:T(2,128)S(1)} %get-tuple-element.445), channel_id=1, source_target_pairs={{8,0},{16,8},{24,16},{9,1},{17,9},{25,17},{10,2},{18,10},{26,18},{... | collective-permute-start | bytes 393224 | tf_op jit(solution)/shard_map/while/body/eval_jaxpr/ppermute | solution.py:17
  224.7 7.5 %collective-permute-start.1 = (f32[2,2,64,128]{3,1,2,0:T(2,128)S(1)}, f32[2,2,64,128]{3,1,2,0:T(2,128)S(1)}, u32[]{:S(2)}, u32[]{:S(2)}) collective-permute-start(f32[2,2,64,128]{3,1,2,0:T(2,128)S(1)} %get-tuple-element.446), channel_id=1, source_target_pairs={{0,8},{8,16},{16,24},{1,9},{9,17},{17,25},{2,10},{10,18},{18,26},{... | collective-permute-start | bytes 393224 | tf_op jit(solution)/shard_map/while/body/eval_jaxpr/ppermute | solution.py:15
  238.0 7.5 %collective-permute-start.4 = (f32[2,8,68,2]{2,1,3,0:T(8,128)S(1)}, f32[2,8,68,2]{2,1,3,0:T(8,128)S(1)}, u32[]{:S(2)}, u32[]{:S(2)}) collective-permute-start(f32[2,8,68,2]{2,1,3,0:T(8,128)S(1)} %copy.101), channel_id=1, source_target_pairs={{1,0},{2,1},{3,2},{5,4},{6,5},{7,6},{9,8},{10,9},{11,10},{13,12},{... | collective-permute-start | bytes 26120 | tf_op jit(solution)/shard_map/while/body/eval_jaxpr/ppermute | solution.py:17
  239.6 7.2 %collective-permute-start.5 = (f32[2,8,68,2]{2,1,3,0:T(8,128)S(1)}, f32[2,8,68,2]{2,1,3,0:T(8,128)S(1)}, u32[]{:S(2)}, u32[]{:S(2)}) collective-permute-start(f32[2,8,68,2]{2,1,3,0:T(8,128)S(1)} %copy.103), channel_id=1, source_target_pairs={{0,1},{1,2},{2,3},{4,5},{5,6},{6,7},{8,9},{9,10},{10,11},{12,13},{... | collective-permute-start | bytes 26120 | tf_op jit(solution)/shard_map/while/body/eval_jaxpr/ppermute | solution.py:15
  250.7 7.5 %collective-permute-start = (f32[2,2,64,128]{3,1,2,0:T(2,128)S(1)}, f32[2,2,64,128]{3,1,2,0:T(2,128)S(1)}, u32[]{:S(2)}, u32[]{:S(2)}) collective-permute-start(f32[2,2,64,128]{3,1,2,0:T(2,128)S(1)} %get-tuple-element.445), channel_id=1, source_target_pairs={{8,0},{16,8},{24,16},{9,1},{17,9},{25,17},{10,2},{18,10},{26,18},{... | collective-permute-start | bytes 393224 | tf_op jit(solution)/shard_map/while/body/eval_jaxpr/ppermute | solution.py:17
  252.0 7.5 %collective-permute-start.1 = (f32[2,2,64,128]{3,1,2,0:T(2,128)S(1)}, f32[2,2,64,128]{3,1,2,0:T(2,128)S(1)}, u32[]{:S(2)}, u32[]{:S(2)}) collective-permute-start(f32[2,2,64,128]{3,1,2,0:T(2,128)S(1)} %get-tuple-element.446), channel_id=1, source_target_pairs={{0,8},{8,16},{16,24},{1,9},{9,17},{17,25},{2,10},{10,18},{18,26},{... | collective-permute-start | bytes 393224 | tf_op jit(solution)/shard_map/while/body/eval_jaxpr/ppermute | solution.py:15
  265.3 7.5 %collective-permute-start.4 = (f32[2,8,68,2]{2,1,3,0:T(8,128)S(1)}, f32[2,8,68,2]{2,1,3,0:T(8,128)S(1)}, u32[]{:S(2)}, u32[]{:S(2)}) collective-permute-start(f32[2,8,68,2]{2,1,3,0:T(8,128)S(1)} %copy.101), channel_id=1, source_target_pairs={{1,0},{2,1},{3,2},{5,4},{6,5},{7,6},{9,8},{10,9},{11,10},{13,12},{... | collective-permute-start | bytes 26120 | tf_op jit(solution)/shard_map/while/body/eval_jaxpr/ppermute | solution.py:17
  266.9 7.2 %collective-permute-start.5 = (f32[2,8,68,2]{2,1,3,0:T(8,128)S(1)}, f32[2,8,68,2]{2,1,3,0:T(8,128)S(1)}, u32[]{:S(2)}, u32[]{:S(2)}) collective-permute-start(f32[2,8,68,2]{2,1,3,0:T(8,128)S(1)} %copy.103), channel_id=1, source_target_pairs={{0,1},{1,2},{2,3},{4,5},{5,6},{6,7},{8,9},{9,10},{10,11},{12,13},{... | collective-permute-start | bytes 26120 | tf_op jit(solution)/shard_map/while/body/eval_jaxpr/ppermute | solution.py:15
  278.0 7.5 %collective-permute-start = (f32[2,2,64,128]{3,1,2,0:T(2,128)S(1)}, f32[2,2,64,128]{3,1,2,0:T(2,128)S(1)}, u32[]{:S(2)}, u32[]{:S(2)}) collective-permute-start(f32[2,2,64,128]{3,1,2,0:T(2,128)S(1)} %get-tuple-element.445), channel_id=1, source_target_pairs={{8,0},{16,8},{24,16},{9,1},{17,9},{25,17},{10,2},{18,10},{26,18},{... | collective-permute-start | bytes 393224 | tf_op jit(solution)/shard_map/while/body/eval_jaxpr/ppermute | solution.py:17
  279.3 7.5 %collective-permute-start.1 = (f32[2,2,64,128]{3,1,2,0:T(2,128)S(1)}, f32[2,2,64,128]{3,1,2,0:T(2,128)S(1)}, u32[]{:S(2)}, u32[]{:S(2)}) collective-permute-start(f32[2,2,64,128]{3,1,2,0:T(2,128)S(1)} %get-tuple-element.446), channel_id=1, source_target_pairs={{0,8},{8,16},{16,24},{1,9},{9,17},{17,25},{2,10},{10,18},{18,26},{... | collective-permute-start | bytes 393224 | tf_op jit(solution)/shard_map/while/body/eval_jaxpr/ppermute | solution.py:15
  292.6 7.5 %collective-permute-start.4 = (f32[2,8,68,2]{2,1,3,0:T(8,128)S(1)}, f32[2,8,68,2]{2,1,3,0:T(8,128)S(1)}, u32[]{:S(2)}, u32[]{:S(2)}) collective-permute-start(f32[2,8,68,2]{2,1,3,0:T(8,128)S(1)} %copy.101), channel_id=1, source_target_pairs={{1,0},{2,1},{3,2},{5,4},{6,5},{7,6},{9,8},{10,9},{11,10},{13,12},{... | collective-permute-start | bytes 26120 | tf_op jit(solution)/shard_map/while/body/eval_jaxpr/ppermute | solution.py:17
  294.2 7.2 %collective-permute-start.5 = (f32[2,8,68,2]{2,1,3,0:T(8,128)S(1)}, f32[2,8,68,2]{2,1,3,0:T(8,128)S(1)}, u32[]{:S(2)}, u32[]{:S(2)}) collective-permute-start(f32[2,8,68,2]{2,1,3,0:T(8,128)S(1)} %copy.103), channel_id=1, source_target_pairs={{0,1},{1,2},{2,3},{4,5},{5,6},{6,7},{8,9},{9,10},{10,11},{12,13},{... | collective-permute-start | bytes 26120 | tf_op jit(solution)/shard_map/while/body/eval_jaxpr/ppermute | solution.py:15
  305.3 7.5 %collective-permute-start = (f32[2,2,64,128]{3,1,2,0:T(2,128)S(1)}, f32[2,2,64,128]{3,1,2,0:T(2,128)S(1)}, u32[]{:S(2)}, u32[]{:S(2)}) collective-permute-start(f32[2,2,64,128]{3,1,2,0:T(2,128)S(1)} %get-tuple-element.445), channel_id=1, source_target_pairs={{8,0},{16,8},{24,16},{9,1},{17,9},{25,17},{10,2},{18,10},{26,18},{... | collective-permute-start | bytes 393224 | tf_op jit(solution)/shard_map/while/body/eval_jaxpr/ppermute | solution.py:17
  306.6 7.5 %collective-permute-start.1 = (f32[2,2,64,128]{3,1,2,0:T(2,128)S(1)}, f32[2,2,64,128]{3,1,2,0:T(2,128)S(1)}, u32[]{:S(2)}, u32[]{:S(2)}) collective-permute-start(f32[2,2,64,128]{3,1,2,0:T(2,128)S(1)} %get-tuple-element.446), channel_id=1, source_target_pairs={{0,8},{8,16},{16,24},{1,9},{9,17},{17,25},{2,10},{10,18},{18,26},{... | collective-permute-start | bytes 393224 | tf_op jit(solution)/shard_map/while/body/eval_jaxpr/ppermute | solution.py:15
  319.9 7.5 %collective-permute-start.4 = (f32[2,8,68,2]{2,1,3,0:T(8,128)S(1)}, f32[2,8,68,2]{2,1,3,0:T(8,128)S(1)}, u32[]{:S(2)}, u32[]{:S(2)}) collective-permute-start(f32[2,8,68,2]{2,1,3,0:T(8,128)S(1)} %copy.101), channel_id=1, source_target_pairs={{1,0},{2,1},{3,2},{5,4},{6,5},{7,6},{9,8},{10,9},{11,10},{13,12},{... | collective-permute-start | bytes 26120 | tf_op jit(solution)/shard_map/while/body/eval_jaxpr/ppermute | solution.py:17
  321.5 7.2 %collective-permute-start.5 = (f32[2,8,68,2]{2,1,3,0:T(8,128)S(1)}, f32[2,8,68,2]{2,1,3,0:T(8,128)S(1)}, u32[]{:S(2)}, u32[]{:S(2)}) collective-permute-start(f32[2,8,68,2]{2,1,3,0:T(8,128)S(1)} %copy.103), channel_id=1, source_target_pairs={{0,1},{1,2},{2,3},{4,5},{5,6},{6,7},{8,9},{9,10},{10,11},{12,13},{... | collective-permute-start | bytes 26120 | tf_op jit(solution)/shard_map/while/body/eval_jaxpr/ppermute | solution.py:15
  332.6 7.5 %collective-permute-start = (f32[2,2,64,128]{3,1,2,0:T(2,128)S(1)}, f32[2,2,64,128]{3,1,2,0:T(2,128)S(1)}, u32[]{:S(2)}, u32[]{:S(2)}) collective-permute-start(f32[2,2,64,128]{3,1,2,0:T(2,128)S(1)} %get-tuple-element.445), channel_id=1, source_target_pairs={{8,0},{16,8},{24,16},{9,1},{17,9},{25,17},{10,2},{18,10},{26,18},{... | collective-permute-start | bytes 393224 | tf_op jit(solution)/shard_map/while/body/eval_jaxpr/ppermute | solution.py:17
  333.9 7.5 %collective-permute-start.1 = (f32[2,2,64,128]{3,1,2,0:T(2,128)S(1)}, f32[2,2,64,128]{3,1,2,0:T(2,128)S(1)}, u32[]{:S(2)}, u32[]{:S(2)}) collective-permute-start(f32[2,2,64,128]{3,1,2,0:T(2,128)S(1)} %get-tuple-element.446), channel_id=1, source_target_pairs={{0,8},{8,16},{16,24},{1,9},{9,17},{17,25},{2,10},{10,18},{18,26},{... | collective-permute-start | bytes 393224 | tf_op jit(solution)/shard_map/while/body/eval_jaxpr/ppermute | solution.py:15
  347.2 7.5 %collective-permute-start.4 = (f32[2,8,68,2]{2,1,3,0:T(8,128)S(1)}, f32[2,8,68,2]{2,1,3,0:T(8,128)S(1)}, u32[]{:S(2)}, u32[]{:S(2)}) collective-permute-start(f32[2,8,68,2]{2,1,3,0:T(8,128)S(1)} %copy.101), channel_id=1, source_target_pairs={{1,0},{2,1},{3,2},{5,4},{6,5},{7,6},{9,8},{10,9},{11,10},{13,12},{... | collective-permute-start | bytes 26120 | tf_op jit(solution)/shard_map/while/body/eval_jaxpr/ppermute | solution.py:17
  348.8 7.2 %collective-permute-start.5 = (f32[2,8,68,2]{2,1,3,0:T(8,128)S(1)}, f32[2,8,68,2]{2,1,3,0:T(8,128)S(1)}, u32[]{:S(2)}, u32[]{:S(2)}) collective-permute-start(f32[2,8,68,2]{2,1,3,0:T(8,128)S(1)} %copy.103), channel_id=1, source_target_pairs={{0,1},{1,2},{2,3},{4,5},{5,6},{6,7},{8,9},{9,10},{10,11},{12,13},{... | collective-permute-start | bytes 26120 | tf_op jit(solution)/shard_map/while/body/eval_jaxpr/ppermute | solution.py:15
  359.9 7.5 %collective-permute-start = (f32[2,2,64,128]{3,1,2,0:T(2,128)S(1)}, f32[2,2,64,128]{3,1,2,0:T(2,128)S(1)}, u32[]{:S(2)}, u32[]{:S(2)}) collective-permute-start(f32[2,2,64,128]{3,1,2,0:T(2,128)S(1)} %get-tuple-element.445), channel_id=1, source_target_pairs={{8,0},{16,8},{24,16},{9,1},{17,9},{25,17},{10,2},{18,10},{26,18},{... | collective-permute-start | bytes 393224 | tf_op jit(solution)/shard_map/while/body/eval_jaxpr/ppermute | solution.py:17
  361.2 7.5 %collective-permute-start.1 = (f32[2,2,64,128]{3,1,2,0:T(2,128)S(1)}, f32[2,2,64,128]{3,1,2,0:T(2,128)S(1)}, u32[]{:S(2)}, u32[]{:S(2)}) collective-permute-start(f32[2,2,64,128]{3,1,2,0:T(2,128)S(1)} %get-tuple-element.446), channel_id=1, source_target_pairs={{0,8},{8,16},{16,24},{1,9},{9,17},{17,25},{2,10},{10,18},{18,26},{... | collective-permute-start | bytes 393224 | tf_op jit(solution)/shard_map/while/body/eval_jaxpr/ppermute | solution.py:15
  374.5 7.5 %collective-permute-start.4 = (f32[2,8,68,2]{2,1,3,0:T(8,128)S(1)}, f32[2,8,68,2]{2,1,3,0:T(8,128)S(1)}, u32[]{:S(2)}, u32[]{:S(2)}) collective-permute-start(f32[2,8,68,2]{2,1,3,0:T(8,128)S(1)} %copy.101), channel_id=1, source_target_pairs={{1,0},{2,1},{3,2},{5,4},{6,5},{7,6},{9,8},{10,9},{11,10},{13,12},{... | collective-permute-start | bytes 26120 | tf_op jit(solution)/shard_map/while/body/eval_jaxpr/ppermute | solution.py:17
  376.1 7.2 %collective-permute-start.5 = (f32[2,8,68,2]{2,1,3,0:T(8,128)S(1)}, f32[2,8,68,2]{2,1,3,0:T(8,128)S(1)}, u32[]{:S(2)}, u32[]{:S(2)}) collective-permute-start(f32[2,8,68,2]{2,1,3,0:T(8,128)S(1)} %copy.103), channel_id=1, source_target_pairs={{0,1},{1,2},{2,3},{4,5},{5,6},{6,7},{8,9},{9,10},{10,11},{12,13},{... | collective-permute-start | bytes 26120 | tf_op jit(solution)/shard_map/while/body/eval_jaxpr/ppermute | solution.py:15
  387.2 7.5 %collective-permute-start = (f32[2,2,64,128]{3,1,2,0:T(2,128)S(1)}, f32[2,2,64,128]{3,1,2,0:T(2,128)S(1)}, u32[]{:S(2)}, u32[]{:S(2)}) collective-permute-start(f32[2,2,64,128]{3,1,2,0:T(2,128)S(1)} %get-tuple-element.445), channel_id=1, source_target_pairs={{8,0},{16,8},{24,16},{9,1},{17,9},{25,17},{10,2},{18,10},{26,18},{... | collective-permute-start | bytes 393224 | tf_op jit(solution)/shard_map/while/body/eval_jaxpr/ppermute | solution.py:17
  388.5 7.5 %collective-permute-start.1 = (f32[2,2,64,128]{3,1,2,0:T(2,128)S(1)}, f32[2,2,64,128]{3,1,2,0:T(2,128)S(1)}, u32[]{:S(2)}, u32[]{:S(2)}) collective-permute-start(f32[2,2,64,128]{3,1,2,0:T(2,128)S(1)} %get-tuple-element.446), channel_id=1, source_target_pairs={{0,8},{8,16},{16,24},{1,9},{9,17},{17,25},{2,10},{10,18},{18,26},{... | collective-permute-start | bytes 393224 | tf_op jit(solution)/shard_map/while/body/eval_jaxpr/ppermute | solution.py:15
  401.8 7.5 %collective-permute-start.4 = (f32[2,8,68,2]{2,1,3,0:T(8,128)S(1)}, f32[2,8,68,2]{2,1,3,0:T(8,128)S(1)}, u32[]{:S(2)}, u32[]{:S(2)}) collective-permute-start(f32[2,8,68,2]{2,1,3,0:T(8,128)S(1)} %copy.101), channel_id=1, source_target_pairs={{1,0},{2,1},{3,2},{5,4},{6,5},{7,6},{9,8},{10,9},{11,10},{13,12},{... | collective-permute-start | bytes 26120 | tf_op jit(solution)/shard_map/while/body/eval_jaxpr/ppermute | solution.py:17
  403.4 7.2 %collective-permute-start.5 = (f32[2,8,68,2]{2,1,3,0:T(8,128)S(1)}, f32[2,8,68,2]{2,1,3,0:T(8,128)S(1)}, u32[]{:S(2)}, u32[]{:S(2)}) collective-permute-start(f32[2,8,68,2]{2,1,3,0:T(8,128)S(1)} %copy.103), channel_id=1, source_target_pairs={{0,1},{1,2},{2,3},{4,5},{5,6},{6,7},{8,9},{9,10},{10,11},{12,13},{... | collective-permute-start | bytes 26120 | tf_op jit(solution)/shard_map/while/body/eval_jaxpr/ppermute | solution.py:15
  414.5 7.5 %collective-permute-start = (f32[2,2,64,128]{3,1,2,0:T(2,128)S(1)}, f32[2,2,64,128]{3,1,2,0:T(2,128)S(1)}, u32[]{:S(2)}, u32[]{:S(2)}) collective-permute-start(f32[2,2,64,128]{3,1,2,0:T(2,128)S(1)} %get-tuple-element.445), channel_id=1, source_target_pairs={{8,0},{16,8},{24,16},{9,1},{17,9},{25,17},{10,2},{18,10},{26,18},{... | collective-permute-start | bytes 393224 | tf_op jit(solution)/shard_map/while/body/eval_jaxpr/ppermute | solution.py:17
  415.8 7.5 %collective-permute-start.1 = (f32[2,2,64,128]{3,1,2,0:T(2,128)S(1)}, f32[2,2,64,128]{3,1,2,0:T(2,128)S(1)}, u32[]{:S(2)}, u32[]{:S(2)}) collective-permute-start(f32[2,2,64,128]{3,1,2,0:T(2,128)S(1)} %get-tuple-element.446), channel_id=1, source_target_pairs={{0,8},{8,16},{16,24},{1,9},{9,17},{17,25},{2,10},{10,18},{18,26},{... | collective-permute-start | bytes 393224 | tf_op jit(solution)/shard_map/while/body/eval_jaxpr/ppermute | solution.py:15
  429.1 7.5 %collective-permute-start.4 = (f32[2,8,68,2]{2,1,3,0:T(8,128)S(1)}, f32[2,8,68,2]{2,1,3,0:T(8,128)S(1)}, u32[]{:S(2)}, u32[]{:S(2)}) collective-permute-start(f32[2,8,68,2]{2,1,3,0:T(8,128)S(1)} %copy.101), channel_id=1, source_target_pairs={{1,0},{2,1},{3,2},{5,4},{6,5},{7,6},{9,8},{10,9},{11,10},{13,12},{... | collective-permute-start | bytes 26120 | tf_op jit(solution)/shard_map/while/body/eval_jaxpr/ppermute | solution.py:17
  430.7 7.2 %collective-permute-start.5 = (f32[2,8,68,2]{2,1,3,0:T(8,128)S(1)}, f32[2,8,68,2]{2,1,3,0:T(8,128)S(1)}, u32[]{:S(2)}, u32[]{:S(2)}) collective-permute-start(f32[2,8,68,2]{2,1,3,0:T(8,128)S(1)} %copy.103), channel_id=1, source_target_pairs={{0,1},{1,2},{2,3},{4,5},{5,6},{6,7},{8,9},{9,10},{10,11},{12,13},{... | collective-permute-start | bytes 26120 | tf_op jit(solution)/shard_map/while/body/eval_jaxpr/ppermute | solution.py:15
  441.8 7.5 %collective-permute-start = (f32[2,2,64,128]{3,1,2,0:T(2,128)S(1)}, f32[2,2,64,128]{3,1,2,0:T(2,128)S(1)}, u32[]{:S(2)}, u32[]{:S(2)}) collective-permute-start(f32[2,2,64,128]{3,1,2,0:T(2,128)S(1)} %get-tuple-element.445), channel_id=1, source_target_pairs={{8,0},{16,8},{24,16},{9,1},{17,9},{25,17},{10,2},{18,10},{26,18},{... | collective-permute-start | bytes 393224 | tf_op jit(solution)/shard_map/while/body/eval_jaxpr/ppermute | solution.py:17
  443.1 7.5 %collective-permute-start.1 = (f32[2,2,64,128]{3,1,2,0:T(2,128)S(1)}, f32[2,2,64,128]{3,1,2,0:T(2,128)S(1)}, u32[]{:S(2)}, u32[]{:S(2)}) collective-permute-start(f32[2,2,64,128]{3,1,2,0:T(2,128)S(1)} %get-tuple-element.446), channel_id=1, source_target_pairs={{0,8},{8,16},{16,24},{1,9},{9,17},{17,25},{2,10},{10,18},{18,26},{... | collective-permute-start | bytes 393224 | tf_op jit(solution)/shard_map/while/body/eval_jaxpr/ppermute | solution.py:15
  456.4 7.5 %collective-permute-start.4 = (f32[2,8,68,2]{2,1,3,0:T(8,128)S(1)}, f32[2,8,68,2]{2,1,3,0:T(8,128)S(1)}, u32[]{:S(2)}, u32[]{:S(2)}) collective-permute-start(f32[2,8,68,2]{2,1,3,0:T(8,128)S(1)} %copy.101), channel_id=1, source_target_pairs={{1,0},{2,1},{3,2},{5,4},{6,5},{7,6},{9,8},{10,9},{11,10},{13,12},{... | collective-permute-start | bytes 26120 | tf_op jit(solution)/shard_map/while/body/eval_jaxpr/ppermute | solution.py:17
  458.0 7.2 %collective-permute-start.5 = (f32[2,8,68,2]{2,1,3,0:T(8,128)S(1)}, f32[2,8,68,2]{2,1,3,0:T(8,128)S(1)}, u32[]{:S(2)}, u32[]{:S(2)}) collective-permute-start(f32[2,8,68,2]{2,1,3,0:T(8,128)S(1)} %copy.103), channel_id=1, source_target_pairs={{0,1},{1,2},{2,3},{4,5},{5,6},{6,7},{8,9},{9,10},{10,11},{12,13},{... | collective-permute-start | bytes 26120 | tf_op jit(solution)/shard_map/while/body/eval_jaxpr/ppermute | solution.py:15
  469.1 7.5 %collective-permute-start = (f32[2,2,64,128]{3,1,2,0:T(2,128)S(1)}, f32[2,2,64,128]{3,1,2,0:T(2,128)S(1)}, u32[]{:S(2)}, u32[]{:S(2)}) collective-permute-start(f32[2,2,64,128]{3,1,2,0:T(2,128)S(1)} %get-tuple-element.445), channel_id=1, source_target_pairs={{8,0},{16,8},{24,16},{9,1},{17,9},{25,17},{10,2},{18,10},{26,18},{... | collective-permute-start | bytes 393224 | tf_op jit(solution)/shard_map/while/body/eval_jaxpr/ppermute | solution.py:17
  470.4 7.5 %collective-permute-start.1 = (f32[2,2,64,128]{3,1,2,0:T(2,128)S(1)}, f32[2,2,64,128]{3,1,2,0:T(2,128)S(1)}, u32[]{:S(2)}, u32[]{:S(2)}) collective-permute-start(f32[2,2,64,128]{3,1,2,0:T(2,128)S(1)} %get-tuple-element.446), channel_id=1, source_target_pairs={{0,8},{8,16},{16,24},{1,9},{9,17},{17,25},{2,10},{10,18},{18,26},{... | collective-permute-start | bytes 393224 | tf_op jit(solution)/shard_map/while/body/eval_jaxpr/ppermute | solution.py:15
  483.7 7.5 %collective-permute-start.4 = (f32[2,8,68,2]{2,1,3,0:T(8,128)S(1)}, f32[2,8,68,2]{2,1,3,0:T(8,128)S(1)}, u32[]{:S(2)}, u32[]{:S(2)}) collective-permute-start(f32[2,8,68,2]{2,1,3,0:T(8,128)S(1)} %copy.101), channel_id=1, source_target_pairs={{1,0},{2,1},{3,2},{5,4},{6,5},{7,6},{9,8},{10,9},{11,10},{13,12},{... | collective-permute-start | bytes 26120 | tf_op jit(solution)/shard_map/while/body/eval_jaxpr/ppermute | solution.py:17
  485.3 7.2 %collective-permute-start.5 = (f32[2,8,68,2]{2,1,3,0:T(8,128)S(1)}, f32[2,8,68,2]{2,1,3,0:T(8,128)S(1)}, u32[]{:S(2)}, u32[]{:S(2)}) collective-permute-start(f32[2,8,68,2]{2,1,3,0:T(8,128)S(1)} %copy.103), channel_id=1, source_target_pairs={{0,1},{1,2},{2,3},{4,5},{5,6},{6,7},{8,9},{9,10},{10,11},{12,13},{... | collective-permute-start | bytes 26120 | tf_op jit(solution)/shard_map/while/body/eval_jaxpr/ppermute | solution.py:15
  496.4 7.5 %collective-permute-start = (f32[2,2,64,128]{3,1,2,0:T(2,128)S(1)}, f32[2,2,64,128]{3,1,2,0:T(2,128)S(1)}, u32[]{:S(2)}, u32[]{:S(2)}) collective-permute-start(f32[2,2,64,128]{3,1,2,0:T(2,128)S(1)} %get-tuple-element.445), channel_id=1, source_target_pairs={{8,0},{16,8},{24,16},{9,1},{17,9},{25,17},{10,2},{18,10},{26,18},{... | collective-permute-start | bytes 393224 | tf_op jit(solution)/shard_map/while/body/eval_jaxpr/ppermute | solution.py:17
  497.7 7.5 %collective-permute-start.1 = (f32[2,2,64,128]{3,1,2,0:T(2,128)S(1)}, f32[2,2,64,128]{3,1,2,0:T(2,128)S(1)}, u32[]{:S(2)}, u32[]{:S(2)}) collective-permute-start(f32[2,2,64,128]{3,1,2,0:T(2,128)S(1)} %get-tuple-element.446), channel_id=1, source_target_pairs={{0,8},{8,16},{16,24},{1,9},{9,17},{17,25},{2,10},{10,18},{18,26},{... | collective-permute-start | bytes 393224 | tf_op jit(solution)/shard_map/while/body/eval_jaxpr/ppermute | solution.py:15
  511.0 7.5 %collective-permute-start.4 = (f32[2,8,68,2]{2,1,3,0:T(8,128)S(1)}, f32[2,8,68,2]{2,1,3,0:T(8,128)S(1)}, u32[]{:S(2)}, u32[]{:S(2)}) collective-permute-start(f32[2,8,68,2]{2,1,3,0:T(8,128)S(1)} %copy.101), channel_id=1, source_target_pairs={{1,0},{2,1},{3,2},{5,4},{6,5},{7,6},{9,8},{10,9},{11,10},{13,12},{... | collective-permute-start | bytes 26120 | tf_op jit(solution)/shard_map/while/body/eval_jaxpr/ppermute | solution.py:17
  512.6 7.2 %collective-permute-start.5 = (f32[2,8,68,2]{2,1,3,0:T(8,128)S(1)}, f32[2,8,68,2]{2,1,3,0:T(8,128)S(1)}, u32[]{:S(2)}, u32[]{:S(2)}) collective-permute-start(f32[2,8,68,2]{2,1,3,0:T(8,128)S(1)} %copy.103), channel_id=1, source_target_pairs={{0,1},{1,2},{2,3},{4,5},{5,6},{6,7},{8,9},{9,10},{10,11},{12,13},{... | collective-permute-start | bytes 26120 | tf_op jit(solution)/shard_map/while/body/eval_jaxpr/ppermute | solution.py:15
  (79 other events, 514.4 us)
where the time goes:
time: 531 us; the launch traced here: 524 us
  starting transfers between devices  302 us (57%)
  waiting for transfers between devices  76.1 us (14%)
  other arithmetic  66.9 us (13%)
  blocking collectives  39.2 us (7%)
  local copies, waits for them, and re-layouts  37.8 us (7%)
    ppermute x53, starting transfers between devices, with_halo(): lax.ppermute(tail, axis, [(i, (i + 1) % count) for i in range(ends)])  233 us
    ppermute x53, starting transfers between devices, with_halo(): lax.ppermute(head, axis, [((i + 1) % count, i) for i in range(ends)])  68.5 us
    ppermute x53, waiting for transfers between devices, with_halo(): lax.ppermute(tail, axis, [(i, (i + 1) % count) for i in range(ends)])  49.2 us
    mul x32, other arithmetic, advance(): return living * updated  30 us
    ppermute x53, waiting for transfers between devices, with_halo(): lax.ppermute(head, axis, [((i + 1) % count, i) for i in range(ends)])  26.9 us
    concatenate x36, other arithmetic, with_halo(): jnp.concatenate([lax.ppermute(tail, axis, [(i, (i + 1) % count) for i in...  20.8 us
    all_gather x1, blocking collectives, local(): cell_rows = lax.all_gather(receiver_cell, 'gx', axis=0, tiled=True)  13.7 us
    all_gather x1, blocking collectives, local(): trace_rows = lax.all_gather(traces, 'gx', axis=0, tiled=True)  13.5 us
  transfers between devices with their start and end apart: 106, of which 67 were waited for; matrix products, arithmetic and copies ran while one was open for 3% of the time, Pallas kernels for 0%

commit v1 on v0

v1 whole, which is shorter than its diff:
```python
import functools

import jax
import jax.numpy as jnp
from jax import lax
from jax.experimental import pallas as pl
from jax.experimental.pallas import tpu as pltpu
from jax.sharding import PartitionSpec as P

MESH = pl.DeviceIdType.MESH
AXES = ("gx", "gy", "gz")


def kernel(
    counts,
    grid_y,
    steps,
    trace_ref,
    tag_ref,
    table_ref,
    top_ref,
    thick_ref,
    courant_ref,
    now_ref,
    before_ref,
    out_ref,
    field,
    ghost_x,
    ghost_y,
    ghost_z,
    send_y,
    send_z,
    living,
    sources,
    traces,
    tags,
    send_sem,
    recv_sem,
    gather_send,
    gather_recv,
):
    tx, ty, tz = courant_ref.shape
    rows = ty // 8
    me = [lax.axis_index(a) for a in AXES]
    has_lo = [me[a] > 0 for a in range(3)]
    has_hi = [me[a] < counts[a] - 1 for a in range(3)]
    lo_id = [{AXES[a]: jnp.maximum(me[a] - 1, 0)} for a in range(3)]
    hi_id = [{AXES[a]: jnp.minimum(me[a] + 1, counts[a] - 1)} for a in range(3)]

    def copy(direction, slot):
        axis, upper = direction // 2, direction % 2
        if axis == 0:
            src = field.at[slot, tx - 1 if upper else 0]
            dst = ghost_x.at[slot, direction % 2]
        elif axis == 1:
            src = send_y.at[slot, upper]
            dst = ghost_y.at[slot, upper]
        else:
            src = send_z.at[slot, upper]
            dst = ghost_z.at[slot, upper]
        return pltpu.make_async_remote_copy(
            src_ref=src,
            dst_ref=dst,
            send_sem=send_sem.at[direction, slot],
            recv_sem=recv_sem.at[direction, slot],
            device_id=(hi_id if upper else lo_id)[axis],
            device_id_type=MESH,
        )

    def target(direction):
        return (has_hi if direction % 2 else has_lo)[direction // 2]

    def origin(direction):
        return (has_lo if direction % 2 else has_hi)[direction // 2]

    def start(direction, slot, also=None):
        cond = target(direction) if also is None else target(direction) & also

        @pl.when(cond)
        def _():
            copy(direction, slot).start()

    def wait_recv(direction, slot):
        @pl.when(origin(direction))
        def _():
            copy(direction, slot).wait_recv()

    def wait_send(direction, slot):
        @pl.when(target(direction))
        def _():
            copy(direction, slot).wait_send()

    ghost_x[...] = jnp.zeros_like(ghost_x)
    ghost_y[...] = jnp.zeros_like(ghost_y)
    ghost_z[...] = jnp.zeros_like(ghost_z)
    field[0] = now_ref[...]
    field[1] = before_ref[...]

    barrier = pltpu.get_barrier_semaphore()
    for d in range(1, counts[0]):
        pl.semaphore_signal(
            barrier,
            inc=1,
            device_id={"gx": lax.rem(me[0] + d, counts[0])},
            device_id_type=MESH,
        )
    for axis in (1, 2):

        @pl.when(has_lo[axis])
        def _():
            pl.semaphore_signal(barrier, inc=1, device_id=lo_id[axis], device_id_type=MESH)

        @pl.when(has_hi[axis])
        def _():
            pl.semaphore_signal(barrier, inc=1, device_id=hi_id[axis], device_id_type=MESH)

    greeted = counts[0] - 1
    for axis in (1, 2):
        greeted = greeted + has_lo[axis].astype(jnp.int32) + has_hi[axis].astype(jnp.int32)

    lane = lax.broadcasted_iota(jnp.int32, (8, tz), 1)

    def pack_z(slot):
        low = jnp.zeros((8, tz), jnp.float32)
        high = jnp.zeros((8, tz), jnp.float32)
        for x in range(tx):
            for b in range(rows):
                j = x * rows + b
                part = field[slot, x, b * 8 : b * 8 + 8, :]
                low = jnp.where(lane == j, pltpu.roll(part, j, 1) if j else part, low)
                high = jnp.where(lane == j, pltpu.roll(part, j + 1, 1), high)
        send_z[slot, 0] = low
        send_z[slot, 1] = high

    def pack_y(slot):
        for x in range(tx):
            send_y[slot, 0, x : x + 1, :] = field[slot, x, 0:1, :]
            send_y[slot, 1, x : x + 1, :] = field[slot, x, ty - 1 : ty, :]

    pack_y(0)
    pack_z(0)
    pl.semaphore_wait(barrier, greeted)
    for direction in range(6):
        start(direction, 0)

    def gather(d):
        there = {"gx": lax.rem(me[0] + d, counts[0])}
        pair = []
        for k, (src, dst) in enumerate(((trace_ref, traces), (tag_ref, tags))):
            pair.append(
                pltpu.make_async_remote_copy(
                    src_ref=src,
                    dst_ref=dst.at[d - 1],
                    send_sem=gather_send.at[d - 1, k],
                    recv_sem=gather_recv.at[d - 1, k],
                    device_id=there,
                    device_id_type=MESH,
                )
            )
        return pair

    for d in range(1, counts[0]):
        for c in gather(d):
            c.start()

    half_y = ty // 2
    pick = lax.broadcasted_iota(jnp.int32, (ty, half_y), 0) // 2 == lax.broadcasted_iota(
        jnp.int32, (ty, half_y), 1
    )
    depth = (me[2] * tz + lax.broadcasted_iota(jnp.int32, (ty, tz), 1)).astype(jnp.float32)
    for xb in range(tx // 2):
        top_row = top_ref[xb : xb + 1, :].astype(jnp.float32)
        thick_row = thick_ref[xb : xb + 1, :].astype(jnp.float32)
        top = jnp.sum(jnp.where(pick, top_row, 0.0), axis=1, keepdims=True)
        end = top + jnp.sum(jnp.where(pick, thick_row, 0.0), axis=1, keepdims=True)
        alive = jnp.where((depth >= top) & (depth < end), 0.0, 1.0)
        living[2 * xb] = alive
        living[2 * xb + 1] = alive

    cells = tx * ty
    row = lax.broadcasted_iota(jnp.int32, (cells, tag_ref.shape[1]), 0)
    surface = (me[2] == 0).astype(jnp.float32)

    def receivers(tag, trace):
        cell = tag[0:1, :]
        kind = tag[1:2, :]
        weight = jnp.zeros(kind.shape, jnp.float32)
        for c in range(table_ref.shape[0]):
            weight = jnp.where(kind == c, table_ref[c], weight)
        x = cell // grid_y - me[0] * tx
        y = cell % grid_y - me[1] * ty
        inside = (x >= 0) & (x < tx) & (y >= 0) & (y < ty)
        seg = jnp.where(inside, x * ty + y, -1)
        hit = row == seg
        total = None
        for _ in range(3):
            piece = weight.astype(jnp.bfloat16).astype(jnp.float32)
            weight = weight - piece
            spread = jnp.where(hit, piece, 0.0).astype(jnp.bfloat16)
            term = lax.dot_general(
                spread, trace, (((1,), (1,)), ((), ())), preferred_element_type=jnp.float32
            )
            total = term if total is None else total + term
        return total

    total = receivers(tag_ref[...], trace_ref[...])
    for d in range(1, counts[0]):
        for c in gather(d):
            c.wait()
        total = total + receivers(tags[d - 1], traces[d - 1])
    total = total * surface
    sources[...] = jnp.zeros_like(sources)
    for x in range(tx):
        sources[x, :, 0:steps] = total[x * ty : (x + 1) * ty]

    wide_lane = lax.broadcasted_iota(jnp.int32, (ty, tz), 1)
    wide_row = lax.broadcasted_iota(jnp.int32, (ty, tz), 0)

    def step(n, slot):
        new = 1 - slot
        more = n < steps - 1
        for direction in (2, 3, 4, 5):
            wait_recv(direction, slot)
        z_low = ghost_z[slot, 1]
        z_high = ghost_z[slot, 0]

        def plane(x, below, above):
            c = field[slot, x]
            y_low = jnp.where(wide_row == 0, ghost_y[slot, 1, x : x + 1, :], pltpu.roll(c, 1, 0))
            y_high = jnp.where(
                wide_row == ty - 1, ghost_y[slot, 0, x : x + 1, :], pltpu.roll(c, ty - 1, 0)
            )
            low_parts, high_parts = [], []
            for b in range(rows):
                j = x * rows + b
                low_parts.append(pltpu.roll(z_low, (tz - j) % tz, 1) if j else z_low)
                high_parts.append(pltpu.roll(z_high, tz - 1 - j, 1))
            left = jnp.where(
                wide_lane == 0, jnp.concatenate(low_parts, axis=0), pltpu.roll(c, 1, 1)
            )
            right = jnp.where(
                wide_lane == tz - 1, jnp.concatenate(high_parts, axis=0), pltpu.roll(c, tz - 1, 1)
            )
            laplace = above + below + y_high + y_low + right + left - 6.0 * c
            source = pltpu.roll(sources[x], lax.rem(n + 1 - steps + tz, tz), 1)
            source = jnp.where(wide_lane == 0, source, 0.0)
            updated = 2.0 * c - field[new, x] + courant_ref[x] * laplace + source
            field[new, x] = living[x] * updated

        for x in range(1, tx - 1):
            plane(x, field[slot, x - 1], field[slot, x + 1])
        wait_recv(1, slot)
        plane(0, ghost_x[slot, 1], field[slot, 1])
        start(0, new, more)
        wait_recv(0, slot)
        plane(tx - 1, field[slot, tx - 2], ghost_x[slot, 0])
        start(1, new, more)
        pack_y(new)
        start(2, new, more)
        start(3, new, more)
        pack_z(new)
        start(4, new, more)
        start(5, new, more)
        for direction in range(6):
            wait_send(direction, slot)

    def double_step(k, carry):
        step(2 * k, 0)
        step(2 * k + 1, 1)
        return carry

    lax.fori_loop(0, steps // 2, double_step, 0)
    out_ref[...] = field[0]


def local(counts, traces, receiver_cell, weight_class, weight_table, top, thick, courant, now, before):
    tx, ty, tz = courant.shape
    count, steps = traces.shape
    tag = jnp.stack([receiver_cell, weight_class])
    others = max(counts[0] - 1, 1)
    vmem = pl.BlockSpec(memory_space=pltpu.VMEM)
    smem = pl.BlockSpec(memory_space=pltpu.SMEM)
    return pl.pallas_call(
        functools.partial(kernel, counts, ty * counts[1], steps),
        out_shape=jax.ShapeDtypeStruct((tx, ty, tz), jnp.float32),
        in_specs=[vmem, vmem, smem, vmem, vmem, vmem, vmem, vmem],
        out_specs=vmem,
        scratch_shapes=[
            pltpu.VMEM((2, tx, ty, tz), jnp.float32),
            pltpu.VMEM((2, 2, ty, tz), jnp.float32),
            pltpu.VMEM((2, 2, tx, tz), jnp.float32),
            pltpu.VMEM((2, 2, 8, tz), jnp.float32),
            pltpu.VMEM((2, 2, tx, tz), jnp.float32),
            pltpu.VMEM((2, 2, 8, tz), jnp.float32),
            pltpu.VMEM((tx, ty, tz), jnp.float32),
            pltpu.VMEM((tx, ty, tz), jnp.float32),
            pltpu.VMEM((others, steps, count), jnp.bfloat16),
            pltpu.VMEM((others, 2, count), jnp.int32),
            pltpu.SemaphoreType.DMA((6, 2)),
            pltpu.SemaphoreType.DMA((6, 2)),
            pltpu.SemaphoreType.DMA((others, 2)),
            pltpu.SemaphoreType.DMA((others, 2)),
        ],
        compiler_params=pltpu.CompilerParams(
            collective_id=0, has_side_effects=True, vmem_limit_bytes=32 * 1024 * 1024
        ),
    )(traces.T, tag, weight_table, top, thick, courant, now, before)


def solution(mesh):
    counts = tuple(mesh.shape[a] for a in AXES)
    tile = P("gx", "gy", "gz")
    columns = P("gx", "gy")
    placed = (P("gx", None), P("gx"), P("gx"), P(), columns, columns, tile, tile, tile)
    return jax.shard_map(
        functools.partial(local, counts), mesh=mesh, in_specs=placed, out_specs=tile, check_vma=False
    )
```

time: 531 us -> 129 us (0.24); the launches traced: 524 us -> 129 us
  starting transfers between devices: 302 us -> 0 us
  Pallas kernels: 0 us -> 123 us
  waiting for transfers between devices: 76.1 us -> 0 us
  other arithmetic: 66.9 us -> 0.01 us
  blocking collectives: 39.2 us -> 0 us
  local copies, waits for them, and re-layouts: 37.8 us -> 5.51 us
    ppermute x106 -> x0, starting transfers between devices: 302 us -> none  [the longest x53 233 us: with_halo(): lax.ppermute(tail, axis, [(i, (i + 1) % count) for i in range(ends)])]
    pallas_call x0 -> x1, Pallas kernels: none -> 123 us  [local(): pl.pallas_call(functools.partial(kernel, counts, ty * counts[1], steps),...]
    ppermute x106 -> x0, waiting for transfers between devices: 76.1 us -> none  [the longest x53 49.2 us: with_halo(): lax.ppermute(tail, axis, [(i, (i + 1) % count) for i in range(ends)])]
    all_gather x3 -> x0, blocking collectives: 39.2 us -> none  [the longest x1 13.7 us: local(): cell_rows = lax.all_gather(receiver_cell, 'gx', axis=0, tiled=True)]
    mul x34 -> x0, other arithmetic: 30 us -> none  [the longest x32 30 us: advance(): return living * updated]
    concatenate x36 -> x0, other arithmetic: 20.8 us -> none  [with_halo(): jnp.concatenate([lax.ppermute(tail, axis, [(i, (i + 1) % count) for i in...]
    slice x87 -> x0, local copies, waits for them, and re-layouts: 15.3 us -> none  [the longest x37 8.27 us: with_halo(): lax.slice_in_dim(cells, cells.shape[dim] - width, cells.shape[dim], axis=...]
    scatter-add x1 -> x0, other arithmetic: 12.9 us -> none  [local(): jax.ops.segment_sum(contrib, segment, num_segments=tile_x * tile_y + 1)]
  transfers between devices with their start and end apart: 106 -> 0, of which waited for: 67 -> 0; matrix products, arithmetic and copies ran while one was open for 3% -> 0% of each run, Pallas kernels for 0% -> 0%
where the time goes in v1:
time: 129 us
  Pallas kernels  123 us (95%)
  local copies, waits for them, and re-layouts  5.51 us (4%)
    pallas_call x1, Pallas kernels, local(): pl.pallas_call(functools.partial(kernel, counts, ty * counts[1], steps),...  123 us
    unnamed x19, local copies, waits for them, and re-layouts  5.51 us

profile of v1, /device:TPU:0, one launch (start us, length us, event | category | flops | bytes accessed | tf_op | source)
XLA Modules:
  0.0 128.9 jit_solution(12878129583091599772)
XLA Ops:
  0.0 0.0 copy-start.8
  0.0 0.0 copy-start.7
  0.0 0.7 copy-done.8
  0.7 0.0 copy-done.7
  0.7 0.0 copy-start.4
  0.7 0.0 copy-start.5
  0.7 0.0 copy-start.6
  0.7 0.7 copy-done.4
  1.4 0.0 copy-done.5
  1.4 0.0 copy-done.6
  1.4 0.0 copy-start
  1.4 0.9 copy-done
  2.3 0.0 copy-start.1
  2.3 0.9 copy-done.1
  3.2 0.0 copy-start.2
  3.2 0.9 copy-done.2
  4.1 0.0 copy-start.3
  4.1 0.8 copy-done.3
  4.9 123.4 %shard_map.91 = f32[4,64,128]{2,1,0:T(8,128)S(1)} custom-call(bf16[32,512]{1,0:T(8,128)(2,1)S(1)} %bitcast.3, s32[2,512]{1,0:T(2,128)S(1)} %pad_add_fusion.tag_ref, f32[16]{0:T(128)S(1)} %copy-done.6, s32[2,32]{1,0:T(2,128)S(1)} %copy-done.4, s32[2,32]{1,0:T(2,128)S(1)} %copy-done.5, f32[4,64,128]{2,1,0:T(8,128)S(1)} %copy-done, ...), custom_call_target="tpu_custom_call" | custom-call | tf_op jit(solution)/shard_map/pallas_call | solution.py:283
  128.2 0.7 copy.11
  (1 shorter events, 0.0 us)
Async XLA Ops:
  0.0 0.7 copy-start.8
  0.0 0.7 copy-start.7
  0.7 0.7 copy-start.4
  0.7 0.7 copy-start.5
  0.7 0.7 copy-start.6
  1.4 0.9 copy-start
  2.3 0.9 copy-start.1
  3.2 0.9 copy-start.2
  4.1 0.8 copy-start.3

commit v2 on v1

--- a/solution.py
+++ b/solution.py
@@ -272,37 +272,392 @@
     lax.fori_loop(0, steps // 2, double_step, 0)
     out_ref[...] = field[0]
 
+DEEP = 8
+
+
+def slab_kernel(
+    counts,
+    grid_y,
+    steps,
+    trace_ref,
+    tag_ref,
+    table_ref,
+    top_ref,
+    thick_ref,
+    courant_ref,
+    now_ref,
+    before_ref,
+    out_ref,
+    field,
+    mine,
+    land_y,
+    land_z,
+    send_z,
+    sources,
+    traces,
+    tags,
+    result,
+    halo_send,
+    halo_recv,
+    swap_send,
+    swap_recv,
+    gather_send,
+    gather_recv,
+    back_send,
+    back_recv,
+):
+    tx, ty, tz = courant_ref.shape
+    nx = counts[0]
+    full_x = tx * nx
+    own = ty // nx
+    rows = own + 2 * DEEP
+    gx, gy, gz = [lax.axis_index(a) for a in AXES]
+
+    def rank_of(x, y):
+        return jnp.where(y % 2 == 0, x, nx - 1 - x)
+
+    place = gy * nx + rank_of(gx, gy)
+    slabs = nx * counts[1]
+
+    hops = [(dy, dz) for dy in (-1, 0, 1) for dz in (-1, 0, 1) if dy or dz]
+
+    def exists(dy, dz):
+        s, z = place + dy, gz + dz
+        return (s >= 0) & (s < slabs) & (z >= 0) & (z < counts[2])
+
+    def device(dy, dz):
+        s = jnp.clip(place + dy, 0, slabs - 1)
+        z = jnp.clip(gz + dz, 0, counts[2] - 1)
+        y = s // nx
+        return (rank_of(s % nx, y), y, z)
+
+    def other(d):
+        return lax.rem(gx + d, nx)
+
+    field[...] = jnp.zeros_like(field)
+    land_y[...] = jnp.zeros_like(land_y)
+    land_z[...] = jnp.zeros_like(land_z)
+
+    barrier = pltpu.get_barrier_semaphore()
+    for d in range(1, nx):
+        pl.semaphore_signal(barrier, inc=1, device_id=(other(d), gy, gz), device_id_type=MESH)
+    greeted = nx - 1
+    for hop in hops:
+        greeted = greeted + exists(*hop).astype(jnp.int32)
+
+        @pl.when(exists(*hop))
+        def _():
+            pl.semaphore_signal(barrier, inc=1, device_id=device(*hop), device_id_type=MESH)
+
+    mine[0] = before_ref[...]
+    mine[1] = now_ref[...]
+    half_y = ty // 2
+    pick = lax.broadcasted_iota(jnp.int32, (ty, half_y), 0) // 2 == lax.broadcasted_iota(
+        jnp.int32, (ty, half_y), 1
+    )
+    depth = (gz * tz + lax.broadcasted_iota(jnp.int32, (ty, tz), 1)).astype(jnp.float32)
+    for xb in range(tx // 2):
+        top_row = top_ref[xb : xb + 1, :].astype(jnp.float32)
+        thick_row = thick_ref[xb : xb + 1, :].astype(jnp.float32)
+        top = jnp.sum(jnp.where(pick, top_row, 0.0), axis=1, keepdims=True)
+        end = top + jnp.sum(jnp.where(pick, thick_row, 0.0), axis=1, keepdims=True)
+        solid = (depth >= top) & (depth < end)
+        for x in (2 * xb, 2 * xb + 1):
+            mine[2, x] = jnp.where(solid, 0.0, courant_ref[x])
+
+    pl.semaphore_wait(barrier, greeted)
+
+    def swap(d):
+        first = pl.multiple_of(rank_of(other(d), gy) * own, 8)
+        return pltpu.make_async_remote_copy(
+            src_ref=mine.at[:, :, pl.ds(first, own), :],
+            dst_ref=field.at[:, pl.ds(gx * tx, tx), pl.ds(DEEP, own), pl.ds(0, tz)],
+            send_sem=swap_send.at[d - 1],
+            recv_sem=swap_recv.at[d - 1],
+            device_id=(other(d), gy, gz),
+            device_id_type=MESH,
+        )
+
+    def gather(d):
+        pair = []
+        for k, (src, dst) in enumerate(((trace_ref, traces), (tag_ref, tags))):
+            pair.append(
+                pltpu.make_async_remote_copy(
+                    src_ref=src,
+                    dst_ref=dst.at[d - 1],
+                    send_sem=gather_send.at[d - 1, k],
+                    recv_sem=gather_recv.at[d - 1, k],
+                    device_id=(other(d), gy, gz),
+                    device_id_type=MESH,
+                )
+            )
+        return pair
+
+    for d in range(1, nx):
+        swap(d).start()
+    for d in range(1, nx):
+        for c in gather(d):
+            c.start()
+    first = pl.multiple_of(rank_of(gx, gy) * own, 8)
+    for x in range(tx):
+        field[:, gx * tx + x, DEEP : DEEP + own, 0:tz] = mine[:, x, pl.ds(first, own), :]
+
+    lane = lax.broadcasted_iota(jnp.int32, (own, tz), 1)
+    tall_lane = lax.broadcasted_iota(jnp.int32, (rows, tz), 1)
+
+    def halo(hop, slot, fields):
+        dy, dz = hop
+        k = hops.index(hop)
+        if dz == 0:
+            src = field.at[
+                pl.ds(0, fields), :, pl.ds(DEEP if dy < 0 else own, DEEP), pl.ds(0, tz)
+            ]
+            dst = land_y.at[slot, 1 if dy < 0 else 0, pl.ds(0, fields)]
+        else:
+            from_row, to_row, size = {
+                -1: (0, DEEP + own, DEEP),
+                0: (0, DEEP, own),
+                1: (own - DEEP, 0, DEEP),
+            }[dy]
+            src = send_z.at[1 if dz > 0 else 0, pl.ds(0, fields), pl.ds(from_row, size)]
+            dst = land_z.at[slot, 1 if dz < 0 else 0, pl.ds(0, fields), pl.ds(to_row, size)]
+        return pltpu.make_async_remote_copy(
+            src_ref=src,
+            dst_ref=dst,
+            send_sem=halo_send.at[k, slot],
+            recv_sem=halo_recv.at[k, slot],
+            device_id=device(dy, dz),
+            device_id_type=MESH,
+        )
+
+    def send_halos(slot, fields):
+        for hop in hops:
+            if hop[1] == 0:
+
+                @pl.when(exists(*hop))
+                def _():
+                    halo(hop, slot, fields).start()
+
+        for f in range(fields):
+            low = jnp.zeros((own, tz), jnp.float32)
+            high = jnp.zeros((own, tz), jnp.float32)
+            for x in range(full_x):
+                part = field[f, x, DEEP : DEEP + own, 0:tz]
+                at = x * DEEP
+                here = (lane >= at) & (lane < at + DEEP)
+                low = jnp.where(here, pltpu.roll(part, at, 1) if at else part, low)
+                turn = (at + DEEP) % tz
+                high = jnp.where(here, pltpu.roll(part, turn, 1) if turn else part, high)
+            send_z[0, f] = low
+            send_z[1, f] = high
+        for hop in hops:
+            if hop[1] != 0:
+
+                @pl.when(exists(*hop))
+                def _():
+                    halo(hop, slot, fields).start()
+
+    def take_halos(slot, fields):
+        for hop in hops:
+
+            @pl.when(exists(-hop[0], -hop[1]))
+            def _():
+                halo(hop, slot, fields).wait_recv()
+
+        for hop in hops:
+
+            @pl.when(exists(*hop))
+            def _():
+                halo(hop, slot, fields).wait_send()
+
+        for f in range(fields):
+            from_low = land_z[slot, 0, f]
+            from_high = land_z[slot, 1, f]
+            for x in range(full_x):
+                field[f, x, 0:DEEP, 0:tz] = land_y[slot, 0, f, x]
+                field[f, x, DEEP + own : rows, 0:tz] = land_y[slot, 1, f, x]
+                right = pltpu.roll(from_high, (tz - x * DEEP) % tz, 1) if x else from_high
+                turn = (2 * tz - DEEP - x * DEEP) % tz
+                left = pltpu.roll(from_low, turn, 1) if turn else from_low
+                field[f, x, :, tz : 2 * tz] = jnp.where(
+                    tall_lane < DEEP, right, jnp.where(tall_lane >= tz - DEEP, left, 0.0)
+                )
+
+    for d in range(1, nx):
+        swap(d).wait()
+    send_halos(0, 3)
+
+    cells = full_x * rows
+    row = lax.broadcasted_iota(jnp.int32, (cells, tag_ref.shape[1]), 0)
+    surface = (gz == 0).astype(jnp.float32)
+
+    def receivers(tag, trace):
+        cell = tag[0:1, :]
+        kind = tag[1:2, :]
+        weight = jnp.zeros(kind.shape, jnp.float32)
+        for c in range(table_ref.shape[0]):
+            weight = jnp.where(kind == c, table_ref[c], weight)
+        y = cell % grid_y - place * own + DEEP
+        seg = jnp.where((y >= 0) & (y < rows), cell // grid_y * rows + y, -1)
+        hit = jnp.where(row == seg, 1.0, 0.0).astype(jnp.bfloat16)
+        left = weight * trace.astype(jnp.float32)
+        total = None
+        for _ in range(3):
+            piece = left.astype(jnp.bfloat16)
+            left = left - piece.astype(jnp.float32)
+            term = lax.dot_general(
+                hit, piece, (((1,), (1,)), ((), ())), preferred_element_type=jnp.float32
+            )
+            total = term if total is None else total + term
+        return total
+
+    total = receivers(tag_ref[...], trace_ref[...])
+    for d in range(1, nx):
+        for c in gather(d):
+            c.wait()
+        total = total + receivers(tags[d - 1], traces[d - 1])
+    total = total * surface
+    sources[...] = jnp.zeros_like(sources)
+    for x in range(full_x):
+        sources[x, :, 0:steps] = total[x * rows : (x + 1) * rows]
+
+    wide = 2 * tz
+
+    def step(n, current):
+        new = 1 - current
+        turn = lax.rem(n + 1 - steps + tz, tz)
+        for x in range(full_x):
+            c = field[current, x]
+            around = pltpu.roll(c, 1, 0) + pltpu.roll(c, rows - 1, 0)
+            around = around + (pltpu.roll(c, 1, 1) + pltpu.roll(c, wide - 1, 1))
+            if x > 0:
+                around = around + field[current, x - 1]
+            if x < full_x - 1:
+                around = around + field[current, x + 1]
+            speed = field[2, x]
+            source = jnp.where(tall_lane == 0, pltpu.roll(sources[x], turn, 1), 0.0)
+            source = jnp.concatenate([source, jnp.zeros_like(source)], axis=1)
+            updated = 2.0 * c - field[new, x] + speed * (around - 6.0 * c) + source
+            field[new, x] = jnp.where(speed > 0.0, updated, 0.0)
+
+    def advance(r):
+        def double_step(k, carry):
+            step(r * DEEP + 2 * k, 1)
+            step(r * DEEP + 2 * k + 1, 0)
+            return carry
+
+        lax.fori_loop(0, DEEP // 2, double_step, 0)
+
+    take_halos(0, 3)
+    advance(0)
+
+    def round_of(r, carry):
+        slot = r % 2
+        send_halos(slot, 2)
+        take_halos(slot, 2)
+        advance(r)
+        return carry
+
+    lax.fori_loop(1, steps // DEEP, round_of, 0)
+
+    def back(d):
+        return pltpu.make_async_remote_copy(
+            src_ref=field.at[1, pl.ds(other(d) * tx, tx), pl.ds(DEEP, own), pl.ds(0, tz)],
+            dst_ref=result.at[:, pl.ds(first, own), :],
+            send_sem=back_send.at[d - 1],
+            recv_sem=back_recv.at[d - 1],
+            device_id=(other(d), gy, gz),
+            device_id_type=MESH,
+        )
+
+    for d in range(1, nx):
+        back(d).start()
+    for x in range(tx):
+        result[x, pl.ds(first, own), :] = field[1, gx * tx + x, DEEP : DEEP + own, 0:tz]
+    for d in range(1, nx):
+        back(d).wait()
+    out_ref[...] = result[...]
+
+
+def slab_scratch(counts, tx, ty, tz, count, steps):
+    nx = counts[0]
+    own = ty // nx
+    rows = own + 2 * DEEP
+    full_x = tx * nx
+    others = max(nx - 1, 1)
+    sem = pltpu.SemaphoreType.DMA
+    return [
+        pltpu.VMEM((3, full_x, rows, 2 * tz), jnp.float32),
+        pltpu.VMEM((3, tx, ty, tz), jnp.float32),
+        pltpu.VMEM((2, 2, 3, full_x, DEEP, tz), jnp.float32),
+        pltpu.VMEM((2, 2, 3, rows, tz), jnp.float32),
+        pltpu.VMEM((2, 3, own, tz), jnp.float32),
+        pltpu.VMEM((full_x, rows, tz), jnp.float32),
+        pltpu.VMEM((others, steps, count), jnp.bfloat16),
+        pltpu.VMEM((others, 2, count), jnp.int32),
+        pltpu.VMEM((tx, ty, tz), jnp.float32),
+        sem((8, 2)),
+        sem((8, 2)),
+        sem((others,)),
+        sem((others,)),
+        sem((others, 2)),
+        sem((others, 2)),
+        sem((others,)),
+        sem((others,)),
+    ]
+
+
+def slabs_fit(counts, tx, ty, tz, steps):
+    own = ty // counts[0]
+    return (
+        own * counts[0] == ty
+        and own % DEEP == 0
+        and tx * counts[0] * DEEP == tz
+        and steps % DEEP == 0
+        and steps <= tz
+    )
+
+
+def face_scratch(counts, tx, ty, tz, count, steps):
+    others = max(counts[0] - 1, 1)
+    return [
+        pltpu.VMEM((2, tx, ty, tz), jnp.float32),
+        pltpu.VMEM((2, 2, ty, tz), jnp.float32),
+        pltpu.VMEM((2, 2, tx, tz), jnp.float32),
+        pltpu.VMEM((2, 2, 8, tz), jnp.float32),
+        pltpu.VMEM((2, 2, tx, tz), jnp.float32),
+        pltpu.VMEM((2, 2, 8, tz), jnp.float32),
+        pltpu.VMEM((tx, ty, tz), jnp.float32),
+        pltpu.VMEM((tx, ty, tz), jnp.float32),
+        pltpu.VMEM((others, steps, count), jnp.bfloat16),
+        pltpu.VMEM((others, 2, count), jnp.int32),
+        pltpu.SemaphoreType.DMA((6, 2)),
+        pltpu.SemaphoreType.DMA((6, 2)),
+        pltpu.SemaphoreType.DMA((others, 2)),
+        pltpu.SemaphoreType.DMA((others, 2)),
+    ]
+
 
 def local(counts, traces, receiver_cell, weight_class, weight_table, top, thick, courant, now, before):
     tx, ty, tz = courant.shape
     count, steps = traces.shape
     tag = jnp.stack([receiver_cell, weight_class])
-    others = max(counts[0] - 1, 1)
     vmem = pl.BlockSpec(memory_space=pltpu.VMEM)
     smem = pl.BlockSpec(memory_space=pltpu.SMEM)
+    if slabs_fit(counts, tx, ty, tz, steps):
+        body, number = slab_kernel, 1
+        scratch = slab_scratch(counts, tx, ty, tz, count, steps)
+    else:
+        body, number = kernel, 0
+        scratch = face_scratch(counts, tx, ty, tz, count, steps)
     return pl.pallas_call(
-        functools.partial(kernel, counts, ty * counts[1], steps),
+        functools.partial(body, counts, ty * counts[1], steps),
         out_shape=jax.ShapeDtypeStruct((tx, ty, tz), jnp.float32),
         in_specs=[vmem, vmem, smem, vmem, vmem, vmem, vmem, vmem],
         out_specs=vmem,
-        scratch_shapes=[
-            pltpu.VMEM((2, tx, ty, tz), jnp.float32),
-            pltpu.VMEM((2, 2, ty, tz), jnp.float32),
-            pltpu.VMEM((2, 2, tx, tz), jnp.float32),
-            pltpu.VMEM((2, 2, 8, tz), jnp.float32),
-            pltpu.VMEM((2, 2, tx, tz), jnp.float32),
-            pltpu.VMEM((2, 2, 8, tz), jnp.float32),
-            pltpu.VMEM((tx, ty, tz), jnp.float32),
-            pltpu.VMEM((tx, ty, tz), jnp.float32),
-            pltpu.VMEM((others, steps, count), jnp.bfloat16),
-            pltpu.VMEM((others, 2, count), jnp.int32),
-            pltpu.SemaphoreType.DMA((6, 2)),
-            pltpu.SemaphoreType.DMA((6, 2)),
-            pltpu.SemaphoreType.DMA((others, 2)),
-            pltpu.SemaphoreType.DMA((others, 2)),
-        ],
+        scratch_shapes=scratch,
         compiler_params=pltpu.CompilerParams(
-            collective_id=0, has_side_effects=True, vmem_limit_bytes=32 * 1024 * 1024
+            collective_id=number, has_side_effects=True, vmem_limit_bytes=32 * 1024 * 1024
         ),
     )(traces.T, tag, weight_table, top, thick, courant, now, before)
 

time: 129 us -> 64.6 us (0.50)
  Pallas kernels: 123 us -> 58.8 us
    pallas_call x1, Pallas kernels: 123 us -> 58.8 us  [local(): pl.pallas_call(functools.partial(body, counts, ty * counts[1], steps), ou...]
where the time goes in v2:
time: 64.6 us; the launch traced here: 64.3 us
  Pallas kernels  58.8 us (91%)
  local copies, waits for them, and re-layouts  5.51 us (9%)
    pallas_call x1, Pallas kernels, local(): pl.pallas_call(functools.partial(body, counts, ty * counts[1], steps), ou...  58.8 us
    unnamed x19, local copies, waits for them, and re-layouts  5.51 us

profile of v2, /device:TPU:0, one launch (start us, length us, event | category | flops | bytes accessed | tf_op | source)
XLA Modules:
  0.0 64.3 jit_solution(10258429301197835201)
XLA Ops:
  0.0 0.0 copy-start.8
  0.0 0.0 copy-start.7
  0.0 0.7 %copy-done.8 = s32[512]{0:T(512)S(1)} copy-done((s32[512]{0:T(512)S(1)}, s32[512]{0:T(512)}, u32[]{:S(2)}) %copy-start.8) | copy-done | bytes 2072
  0.7 0.0 copy-done.7
  0.7 0.0 copy-start.4
  0.7 0.0 copy-start.5
  0.7 0.0 copy-start.6
  0.7 0.7 %copy-done.4 = s32[2,32]{1,0:T(2,128)S(1)} copy-done((s32[2,32]{1,0:T(2,128)S(1)}, s32[2,32]{1,0:T(2,128)}, u32[]{:S(2)}) %copy-start.4) | copy-done | bytes 280
  1.4 0.0 copy-done.5
  1.4 0.0 copy-done.6
  1.4 0.0 copy-start
  1.4 0.9 %copy-done = f32[4,64,128]{2,1,0:T(8,128)S(1)} copy-done((f32[4,64,128]{2,1,0:T(8,128)S(1)}, f32[4,64,128]{2,1,0:T(8,128)}, u32[]{:S(2)}) %copy-start) | copy-done | bytes 131096
  2.3 0.0 copy-start.1
  2.3 0.9 %copy-done.1 = f32[4,64,128]{2,1,0:T(8,128)S(1)} copy-done((f32[4,64,128]{2,1,0:T(8,128)S(1)}, f32[4,64,128]{2,1,0:T(8,128)}, u32[]{:S(2)}) %copy-start.1) | copy-done | bytes 131096
  3.2 0.0 copy-start.2
  3.2 0.9 %copy-done.2 = f32[4,64,128]{2,1,0:T(8,128)S(1)} copy-done((f32[4,64,128]{2,1,0:T(8,128)S(1)}, f32[4,64,128]{2,1,0:T(8,128)}, u32[]{:S(2)}) %copy-start.2) | copy-done | bytes 131096
  4.1 0.0 copy-start.3
  4.1 0.8 %copy-done.3 = bf16[512,32]{0,1:T(8,128)(2,1)S(1)} copy-done((bf16[512,32]{0,1:T(8,128)(2,1)S(1)}, bf16[512,32]{0,1:T(8,128)(2,1)}, u32[]{:S(2)}) %copy-start.3) | copy-done | bytes 32792
  4.9 58.8 %shard_map.91 = f32[4,64,128]{2,1,0:T(8,128)S(1)} custom-call(bf16[32,512]{1,0:T(8,128)(2,1)S(1)} %bitcast.3, s32[2,512]{1,0:T(2,128)S(1)} %pad_add_fusion.tag_ref, f32[16]{0:T(128)S(1)} %copy-done.6, s32[2,32]{1,0:T(2,128)S(1)} %copy-done.4, s32[2,32]{1,0:T(2,128)S(1)} %copy-done.5, f32[4,64,128]{2,1,0:T(8,128)S(1)} %copy-done, ...), custom_call_target="tpu_custom_call" | custom-call | tf_op jit(solution)/shard_map/pallas_call | solution.py:653
  63.6 0.7 %copy.11 = f32[4,64,128]{2,1,0:T(8,128)} copy(f32[4,64,128]{2,1,0:T(8,128)S(1)} %shard_map.91) | data formatting | bytes 262144
  (1 shorter events, 0.0 us)
Async XLA Ops:
  0.0 0.7 %copy-start.8 = (s32[512]{0:T(512)S(1)}, s32[512]{0:T(512)}, u32[]{:S(2)}) copy-start(s32[512]{0:T(512)} %param.10) | copy-start | bytes 6148
  0.0 0.7 %copy-start.7 = (s32[512]{0:T(512)S(1)}, s32[512]{0:T(512)}, u32[]{:S(2)}) copy-start(s32[512]{0:T(512)} %param.11) | copy-start | bytes 6148
  0.7 0.7 %copy-start.4 = (s32[2,32]{1,0:T(2,128)S(1)}, s32[2,32]{1,0:T(2,128)}, u32[]{:S(2)}) copy-start(s32[2,32]{1,0:T(2,128)} %top_ref.1) | copy-start | bytes 772
  0.7 0.7 %copy-start.5 = (s32[2,32]{1,0:T(2,128)S(1)}, s32[2,32]{1,0:T(2,128)}, u32[]{:S(2)}) copy-start(s32[2,32]{1,0:T(2,128)} %thick_ref.1) | copy-start | bytes 772
  0.7 0.7 %copy-start.6 = (f32[16]{0:T(128)S(1)}, f32[16]{0:T(128)}, u32[]{:S(2)}) copy-start(f32[16]{0:T(128)} %table_ref.1) | copy-start | bytes 196
  1.4 0.9 %copy-start = (f32[4,64,128]{2,1,0:T(8,128)S(1)}, f32[4,64,128]{2,1,0:T(8,128)}, u32[]{:S(2)}) copy-start(f32[4,64,128]{2,1,0:T(8,128)} %courant_ref.1) | copy-start | bytes 393220
  2.3 0.9 %copy-start.1 = (f32[4,64,128]{2,1,0:T(8,128)S(1)}, f32[4,64,128]{2,1,0:T(8,128)}, u32[]{:S(2)}) copy-start(f32[4,64,128]{2,1,0:T(8,128)} %now_ref.1) | copy-start | bytes 393220
  3.2 0.9 %copy-start.2 = (f32[4,64,128]{2,1,0:T(8,128)S(1)}, f32[4,64,128]{2,1,0:T(8,128)}, u32[]{:S(2)}) copy-start(f32[4,64,128]{2,1,0:T(8,128)} %before_ref.1) | copy-start | bytes 393220
  4.1 0.8 %copy-start.3 = (bf16[512,32]{0,1:T(8,128)(2,1)S(1)}, bf16[512,32]{0,1:T(8,128)(2,1)}, u32[]{:S(2)}) copy-start(bf16[512,32]{0,1:T(8,128)(2,1)} %param.9) | copy-start | bytes 98308

commit v3 on v2

--- a/solution.py
+++ b/solution.py
@@ -305,6 +305,9 @@
     gather_recv,
     back_send,
     back_recv,
+    tops,
+    thicks,
+    fetch_sem,
 ):
     tx, ty, tz = courant_ref.shape
     nx = counts[0]
@@ -313,11 +316,24 @@
     rows = own + 2 * DEEP
     gx, gy, gz = [lax.axis_index(a) for a in AXES]
 
-    def rank_of(x, y):
-        return jnp.where(y % 2 == 0, x, nx - 1 - x)
-
-    place = gy * nx + rank_of(gx, gy)
-    slabs = nx * counts[1]
+    ny = counts[1]
+    slabs = nx * ny
+    place = gx * ny + gy
+    source_y = place // nx
+    my_part = place % nx
+    inner = source_y == gy
+
+    def slab_device(s, z):
+        return (s // ny, s % ny, z)
+
+    def target(t):
+        return slab_device(gy * nx + t, gz)
+
+    def apart(t):
+        return gy * nx + t != place
+
+    def distant(i):
+        return (gx != i) | (gy != source_y)
 
     hops = [(dy, dz) for dy in (-1, 0, 1) for dz in (-1, 0, 1) if dy or dz]
 
@@ -328,20 +344,49 @@
     def device(dy, dz):
         s = jnp.clip(place + dy, 0, slabs - 1)
         z = jnp.clip(gz + dz, 0, counts[2] - 1)
-        y = s // nx
-        return (rank_of(s % nx, y), y, z)
+        return slab_device(s, z)
 
     def other(d):
         return lax.rem(gx + d, nx)
+
+    fetches = [
+        pltpu.make_async_copy(src, dst, fetch_sem.at[i])
+        for i, (src, dst) in enumerate(
+            (
+                (courant_ref, mine.at[2]),
+                (top_ref, tops),
+                (thick_ref, thicks),
+                (before_ref, mine.at[0]),
+                (now_ref, mine.at[1]),
+            )
+        )
+    ]
+    for c in fetches:
+        c.start()
 
     field[...] = jnp.zeros_like(field)
     land_y[...] = jnp.zeros_like(land_y)
     land_z[...] = jnp.zeros_like(land_z)
 
     barrier = pltpu.get_barrier_semaphore()
+    on_top = gz == 0
+    own_receivers = [
+        pltpu.make_async_copy(trace_ref, traces.at[0], gather_send.at[0, 0]),
+        pltpu.make_async_copy(tag_ref, tags.at[0], gather_send.at[0, 1]),
+    ]
     for d in range(1, nx):
         pl.semaphore_signal(barrier, inc=1, device_id=(other(d), gy, gz), device_id_type=MESH)
-    greeted = nx - 1
+    for t in range(nx):
+
+        @pl.when(apart(t))
+        def _():
+            pl.semaphore_signal(barrier, inc=1, device_id=target(t), device_id_type=MESH)
+
+        @pl.when(distant(t))
+        def _():
+            pl.semaphore_signal(barrier, inc=1, device_id=(t, source_y, gz), device_id_type=MESH)
+
+    greeted = nx - 1 + 2 * (nx - inner.astype(jnp.int32))
     for hop in hops:
         greeted = greeted + exists(*hop).astype(jnp.int32)
 
@@ -349,32 +394,33 @@
         def _():
             pl.semaphore_signal(barrier, inc=1, device_id=device(*hop), device_id_type=MESH)
 
-    mine[0] = before_ref[...]
-    mine[1] = now_ref[...]
+    for c in own_receivers:
+        c.start()
+    for c in fetches:
+        c.wait()
     half_y = ty // 2
     pick = lax.broadcasted_iota(jnp.int32, (ty, half_y), 0) // 2 == lax.broadcasted_iota(
         jnp.int32, (ty, half_y), 1
     )
     depth = (gz * tz + lax.broadcasted_iota(jnp.int32, (ty, tz), 1)).astype(jnp.float32)
     for xb in range(tx // 2):
-        top_row = top_ref[xb : xb + 1, :].astype(jnp.float32)
-        thick_row = thick_ref[xb : xb + 1, :].astype(jnp.float32)
+        top_row = tops[xb : xb + 1, :].astype(jnp.float32)
+        thick_row = thicks[xb : xb + 1, :].astype(jnp.float32)
         top = jnp.sum(jnp.where(pick, top_row, 0.0), axis=1, keepdims=True)
         end = top + jnp.sum(jnp.where(pick, thick_row, 0.0), axis=1, keepdims=True)
         solid = (depth >= top) & (depth < end)
         for x in (2 * xb, 2 * xb + 1):
-            mine[2, x] = jnp.where(solid, 0.0, courant_ref[x])
+            mine[2, x] = jnp.where(solid, 0.0, mine[2, x])
 
     pl.semaphore_wait(barrier, greeted)
 
-    def swap(d):
-        first = pl.multiple_of(rank_of(other(d), gy) * own, 8)
+    def swap(t, i):
         return pltpu.make_async_remote_copy(
-            src_ref=mine.at[:, :, pl.ds(first, own), :],
+            src_ref=mine.at[:, :, pl.ds(t * own, own), :],
             dst_ref=field.at[:, pl.ds(gx * tx, tx), pl.ds(DEEP, own), pl.ds(0, tz)],
-            send_sem=swap_send.at[d - 1],
-            recv_sem=swap_recv.at[d - 1],
-            device_id=(other(d), gy, gz),
+            send_sem=swap_send.at[t],
+            recv_sem=swap_recv.at[i],
+            device_id=target(t),
             device_id_type=MESH,
         )
 
@@ -384,23 +430,33 @@
             pair.append(
                 pltpu.make_async_remote_copy(
                     src_ref=src,
-                    dst_ref=dst.at[d - 1],
-                    send_sem=gather_send.at[d - 1, k],
-                    recv_sem=gather_recv.at[d - 1, k],
+                    dst_ref=dst.at[d],
+                    send_sem=gather_send.at[d, k],
+                    recv_sem=gather_recv.at[d, k],
                     device_id=(other(d), gy, gz),
                     device_id_type=MESH,
                 )
             )
         return pair
 
-    for d in range(1, nx):
-        swap(d).start()
-    for d in range(1, nx):
-        for c in gather(d):
-            c.start()
-    first = pl.multiple_of(rank_of(gx, gy) * own, 8)
-    for x in range(tx):
-        field[:, gx * tx + x, DEEP : DEEP + own, 0:tz] = mine[:, x, pl.ds(first, own), :]
+    for t in range(nx):
+
+        @pl.when(apart(t))
+        def _():
+            swap(t, gx).start()
+
+    @pl.when(on_top)
+    def _():
+        for d in range(1, nx):
+            for c in gather(d):
+                c.start()
+
+    first = pl.multiple_of(my_part * own, 8)
+
+    @pl.when(inner)
+    def _():
+        for x in range(tx):
+            field[:, gx * tx + x, DEEP : DEEP + own, 0:tz] = mine[:, x, pl.ds(first, own), :]
 
     lane = lax.broadcasted_iota(jnp.int32, (own, tz), 1)
     tall_lane = lax.broadcasted_iota(jnp.int32, (rows, tz), 1)
@@ -483,13 +539,16 @@
                     tall_lane < DEEP, right, jnp.where(tall_lane >= tz - DEEP, left, 0.0)
                 )
 
-    for d in range(1, nx):
-        swap(d).wait()
+    for i in range(nx):
+
+        @pl.when(distant(i))
+        def _():
+            swap(0, i).wait_recv()
+
     send_halos(0, 3)
 
     cells = full_x * rows
     row = lax.broadcasted_iota(jnp.int32, (cells, tag_ref.shape[1]), 0)
-    surface = (gz == 0).astype(jnp.float32)
 
     def receivers(tag, trace):
         cell = tag[0:1, :]
@@ -511,15 +570,25 @@
             total = term if total is None else total + term
         return total
 
-    total = receivers(tag_ref[...], trace_ref[...])
-    for d in range(1, nx):
-        for c in gather(d):
-            c.wait()
-        total = total + receivers(tags[d - 1], traces[d - 1])
-    total = total * surface
     sources[...] = jnp.zeros_like(sources)
-    for x in range(full_x):
-        sources[x, :, 0:steps] = total[x * rows : (x + 1) * rows]
+    for c in own_receivers:
+        c.wait()
+
+    @pl.when(on_top)
+    def _():
+        total = receivers(tags[0], traces[0])
+        for d in range(1, nx):
+            for c in gather(d):
+                c.wait()
+            total = total + receivers(tags[d], traces[d])
+        for x in range(full_x):
+            sources[x, :, 0:steps] = total[x * rows : (x + 1) * rows]
+
+    for t in range(nx):
+
+        @pl.when(apart(t))
+        def _():
+            swap(t, gx).wait_send()
 
     wide = 2 * tz
 
@@ -560,22 +629,39 @@
 
     lax.fori_loop(1, steps // DEEP, round_of, 0)
 
-    def back(d):
+    def back(i, part):
         return pltpu.make_async_remote_copy(
-            src_ref=field.at[1, pl.ds(other(d) * tx, tx), pl.ds(DEEP, own), pl.ds(0, tz)],
+            src_ref=field.at[1, pl.ds(i * tx, tx), pl.ds(DEEP, own), pl.ds(0, tz)],
             dst_ref=result.at[:, pl.ds(first, own), :],
-            send_sem=back_send.at[d - 1],
-            recv_sem=back_recv.at[d - 1],
-            device_id=(other(d), gy, gz),
+            send_sem=back_send.at[i],
+            recv_sem=back_recv.at[part],
+            device_id=(i, source_y, gz),
             device_id_type=MESH,
         )
 
-    for d in range(1, nx):
-        back(d).start()
-    for x in range(tx):
-        result[x, pl.ds(first, own), :] = field[1, gx * tx + x, DEEP : DEEP + own, 0:tz]
-    for d in range(1, nx):
-        back(d).wait()
+    for i in range(nx):
+
+        @pl.when(distant(i))
+        def _():
+            back(i, my_part).start()
+
+    @pl.when(inner)
+    def _():
+        for x in range(tx):
+            result[x, pl.ds(first, own), :] = field[1, gx * tx + x, DEEP : DEEP + own, 0:tz]
+
+    for t in range(nx):
+
+        @pl.when(apart(t))
+        def _():
+            back(0, t).wait_recv()
+
+    for i in range(nx):
+
+        @pl.when(distant(i))
+        def _():
+            back(i, my_part).wait_send()
+
     out_ref[...] = result[...]
 
 
@@ -584,7 +670,6 @@
     own = ty // nx
     rows = own + 2 * DEEP
     full_x = tx * nx
-    others = max(nx - 1, 1)
     sem = pltpu.SemaphoreType.DMA
     return [
         pltpu.VMEM((3, full_x, rows, 2 * tz), jnp.float32),
@@ -593,17 +678,20 @@
         pltpu.VMEM((2, 2, 3, rows, tz), jnp.float32),
         pltpu.VMEM((2, 3, own, tz), jnp.float32),
         pltpu.VMEM((full_x, rows, tz), jnp.float32),
-        pltpu.VMEM((others, steps, count), jnp.bfloat16),
-        pltpu.VMEM((others, 2, count), jnp.int32),
+        pltpu.VMEM((nx, steps, count), jnp.bfloat16),
+        pltpu.VMEM((nx, 2, count), jnp.int32),
         pltpu.VMEM((tx, ty, tz), jnp.float32),
         sem((8, 2)),
         sem((8, 2)),
-        sem((others,)),
-        sem((others,)),
-        sem((others, 2)),
-        sem((others, 2)),
-        sem((others,)),
-        sem((others,)),
+        sem((nx,)),
+        sem((nx,)),
+        sem((nx, 2)),
+        sem((nx, 2)),
+        sem((nx,)),
+        sem((nx,)),
+        pltpu.VMEM((tx // 2, ty // 2), jnp.int32),
+        pltpu.VMEM((tx // 2, ty // 2), jnp.int32),
+        sem((5,)),
     ]
 
 
@@ -645,19 +733,19 @@
     vmem = pl.BlockSpec(memory_space=pltpu.VMEM)
     smem = pl.BlockSpec(memory_space=pltpu.SMEM)
     if slabs_fit(counts, tx, ty, tz, steps):
-        body, number = slab_kernel, 1
+        body, number, place = slab_kernel, 1, pl.BlockSpec(memory_space=pl.ANY)
         scratch = slab_scratch(counts, tx, ty, tz, count, steps)
     else:
-        body, number = kernel, 0
+        body, number, place = kernel, 0, vmem
         scratch = face_scratch(counts, tx, ty, tz, count, steps)
     return pl.pallas_call(
         functools.partial(body, counts, ty * counts[1], steps),
         out_shape=jax.ShapeDtypeStruct((tx, ty, tz), jnp.float32),
-        in_specs=[vmem, vmem, smem, vmem, vmem, vmem, vmem, vmem],
+        in_specs=[place, place, smem, place, place, place, place, place],
         out_specs=vmem,
         scratch_shapes=scratch,
         compiler_params=pltpu.CompilerParams(
-            collective_id=number, has_side_effects=True, vmem_limit_bytes=32 * 1024 * 1024
+            collective_id=number, has_side_effects=True, vmem_limit_bytes=56 * 1024 * 1024
         ),
     )(traces.T, tag, weight_table, top, thick, courant, now, before)
 

time: 64.6 us -> 58.6 us (0.907)
  Pallas kernels: 58.8 us -> 55.5 us
  local copies, waits for them, and re-layouts: 5.51 us -> 2.26 us
    pallas_call x1, Pallas kernels: 58.8 us -> 55.5 us  [local(): pl.pallas_call(functools.partial(body, counts, ty * counts[1], steps), ou...]
    unnamed x19 -> x5, local copies, waits for them, and re-layouts: 5.51 us -> 2.26 us
where the time goes in v3:
time: 58.6 us; the launch traced here: 58.4 us
  Pallas kernels  55.5 us (95%)
  local copies, waits for them, and re-layouts  2.26 us (4%)
  other arithmetic  0.6 us (1%)
    pallas_call x1, Pallas kernels, local(): pl.pallas_call(functools.partial(body, counts, ty * counts[1], steps), ou...  55.5 us
    unnamed x5, local copies, waits for them, and re-layouts  2.26 us

profile of v3, /device:TPU:0, one launch (start us, length us, event | category | flops | bytes accessed | tf_op | source)
XLA Modules:
  0.0 58.4 jit_solution(16514854655131239762)
XLA Ops:
  0.0 0.0 copy-start.1
  0.0 0.0 copy-start
  0.0 0.7 %copy-done.1 = s32[512]{0:T(512)S(1)} copy-done((s32[512]{0:T(512)S(1)}, s32[512]{0:T(512)}, u32[]{:S(2)}) %copy-start.1) | copy-done | bytes 2072
  0.7 0.0 copy-done
  0.7 0.6 %pad_add_fusion.tag_ref = s32[2,512]{1,0:T(2,128)} fusion(s32[1,512]{1,0:T(1,128)S(1)} %bitcast.4, s32[1,512]{1,0:T(1,128)S(1)} %bitcast.5), kind=kLoop, calls=%fused_computation | loop fusion | flops 1024 | bytes 8192 | tf_op jit(solution)/shard_map/stack | solution.py:732
  1.3 55.5 %shard_map.91 = f32[4,64,128]{2,1,0:T(8,128)} custom-call(bf16[32,512]{1,0:T(8,128)(2,1)} %bitcast.3, s32[2,512]{1,0:T(2,128)} %pad_add_fusion.tag_ref, f32[16]{0:T(128)} %table_ref.1, s32[2,32]{1,0:T(2,128)} %top_ref.1, s32[2,32]{1,0:T(2,128)} %thick_ref.1, f32[4,64,128]{2,1,0:T(8,128)} %courant_ref.1, f32[4,64,128]{2,1,0:T(8,128)} %now_ref.1, ...), custom_call_target="tpu_custom_call" | custom-call | tf_op jit(solution)/shard_map/pallas_call | solution.py:741
  56.8 1.6 %copy.11 = f32[4,64,128]{2,1,0:T(8,128)} copy(f32[4,64,128]{2,1,0:T(8,128)} %shard_map.91) | data formatting | bytes 262144
Async XLA Ops:
  0.0 0.7 %copy-start.1 = (s32[512]{0:T(512)S(1)}, s32[512]{0:T(512)}, u32[]{:S(2)}) copy-start(s32[512]{0:T(512)} %param.10) | copy-start | bytes 6148
  0.0 0.7 %copy-start = (s32[512]{0:T(512)S(1)}, s32[512]{0:T(512)}, u32[]{:S(2)}) copy-start(s32[512]{0:T(512)} %param.11) | copy-start | bytes 6148

commit v4 on v3

--- a/solution.py
+++ b/solution.py
@@ -280,7 +280,8 @@
     grid_y,
     steps,
     trace_ref,
-    tag_ref,
+    cell_ref,
+    class_ref,
     table_ref,
     top_ref,
     thick_ref,
@@ -295,7 +296,8 @@
     send_z,
     sources,
     traces,
-    tags,
+    cell_rows,
+    class_rows,
     result,
     halo_send,
     halo_recv,
@@ -353,11 +355,11 @@
         pltpu.make_async_copy(src, dst, fetch_sem.at[i])
         for i, (src, dst) in enumerate(
             (
-                (courant_ref, mine.at[2]),
+                (before_ref, mine.at[0]),
+                (now_ref, mine.at[1]),
                 (top_ref, tops),
                 (thick_ref, thicks),
-                (before_ref, mine.at[0]),
-                (now_ref, mine.at[1]),
+                (courant_ref, mine.at[2]),
             )
         )
     ]
@@ -372,7 +374,8 @@
     on_top = gz == 0
     own_receivers = [
         pltpu.make_async_copy(trace_ref, traces.at[0], gather_send.at[0, 0]),
-        pltpu.make_async_copy(tag_ref, tags.at[0], gather_send.at[0, 1]),
+        pltpu.make_async_copy(cell_ref, cell_rows.at[0], gather_send.at[0, 1]),
+        pltpu.make_async_copy(class_ref, class_rows.at[0], gather_send.at[0, 2]),
     ]
     for d in range(1, nx):
         pl.semaphore_signal(barrier, inc=1, device_id=(other(d), gy, gz), device_id_type=MESH)
@@ -396,7 +399,49 @@
 
     for c in own_receivers:
         c.start()
-    for c in fetches:
+    for c in fetches[:2]:
+        c.wait()
+    pl.semaphore_wait(barrier, greeted)
+
+    def swap(t, i, part):
+        some = pl.ds(2 * part, 2 - part)
+        return pltpu.make_async_remote_copy(
+            src_ref=mine.at[some, :, pl.ds(t * own, own), :],
+            dst_ref=field.at[some, pl.ds(gx * tx, tx), pl.ds(DEEP, own), pl.ds(0, tz)],
+            send_sem=swap_send.at[t, part],
+            recv_sem=swap_recv.at[i, part],
+            device_id=target(t),
+            device_id_type=MESH,
+        )
+
+    def gather(d):
+        pair = []
+        for k, (src, dst) in enumerate(((trace_ref, traces), (cell_ref, cell_rows), (class_ref, class_rows))):
+            pair.append(
+                pltpu.make_async_remote_copy(
+                    src_ref=src,
+                    dst_ref=dst.at[d],
+                    send_sem=gather_send.at[d, k],
+                    recv_sem=gather_recv.at[d, k],
+                    device_id=(other(d), gy, gz),
+                    device_id_type=MESH,
+                )
+            )
+        return pair
+
+    for t in range(nx):
+
+        @pl.when(apart(t))
+        def _():
+            swap(t, gx, 0).start()
+
+    @pl.when(on_top)
+    def _():
+        for d in range(1, nx):
+            for c in gather(d):
+                c.start()
+
+    for c in fetches[2:]:
         c.wait()
     half_y = ty // 2
     pick = lax.broadcasted_iota(jnp.int32, (ty, half_y), 0) // 2 == lax.broadcasted_iota(
@@ -412,44 +457,11 @@
         for x in (2 * xb, 2 * xb + 1):
             mine[2, x] = jnp.where(solid, 0.0, mine[2, x])
 
-    pl.semaphore_wait(barrier, greeted)
-
-    def swap(t, i):
-        return pltpu.make_async_remote_copy(
-            src_ref=mine.at[:, :, pl.ds(t * own, own), :],
-            dst_ref=field.at[:, pl.ds(gx * tx, tx), pl.ds(DEEP, own), pl.ds(0, tz)],
-            send_sem=swap_send.at[t],
-            recv_sem=swap_recv.at[i],
-            device_id=target(t),
-            device_id_type=MESH,
-        )
-
-    def gather(d):
-        pair = []
-        for k, (src, dst) in enumerate(((trace_ref, traces), (tag_ref, tags))):
-            pair.append(
-                pltpu.make_async_remote_copy(
-                    src_ref=src,
-                    dst_ref=dst.at[d],
-                    send_sem=gather_send.at[d, k],
-                    recv_sem=gather_recv.at[d, k],
-                    device_id=(other(d), gy, gz),
-                    device_id_type=MESH,
-                )
-            )
-        return pair
-
     for t in range(nx):
 
         @pl.when(apart(t))
         def _():
-            swap(t, gx).start()
-
-    @pl.when(on_top)
-    def _():
-        for d in range(1, nx):
-            for c in gather(d):
-                c.start()
+            swap(t, gx, 1).start()
 
     first = pl.multiple_of(my_part * own, 8)
 
@@ -461,40 +473,41 @@
     lane = lax.broadcasted_iota(jnp.int32, (own, tz), 1)
     tall_lane = lax.broadcasted_iota(jnp.int32, (rows, tz), 1)
 
-    def halo(hop, slot, fields):
+    def halo(hop, slot, low_field, fields, sem):
         dy, dz = hop
         k = hops.index(hop)
+        some = pl.ds(low_field, fields)
         if dz == 0:
             src = field.at[
-                pl.ds(0, fields), :, pl.ds(DEEP if dy < 0 else own, DEEP), pl.ds(0, tz)
+                pl.ds(low_field, fields), :, pl.ds(DEEP if dy < 0 else own, DEEP), pl.ds(0, tz)
             ]
-            dst = land_y.at[slot, 1 if dy < 0 else 0, pl.ds(0, fields)]
+            dst = land_y.at[slot, 1 if dy < 0 else 0, pl.ds(low_field, fields)]
         else:
             from_row, to_row, size = {
                 -1: (0, DEEP + own, DEEP),
                 0: (0, DEEP, own),
                 1: (own - DEEP, 0, DEEP),
             }[dy]
-            src = send_z.at[1 if dz > 0 else 0, pl.ds(0, fields), pl.ds(from_row, size)]
-            dst = land_z.at[slot, 1 if dz < 0 else 0, pl.ds(0, fields), pl.ds(to_row, size)]
+            src = send_z.at[1 if dz > 0 else 0, some, pl.ds(from_row, size)]
+            dst = land_z.at[slot, 1 if dz < 0 else 0, some, pl.ds(to_row, size)]
         return pltpu.make_async_remote_copy(
             src_ref=src,
             dst_ref=dst,
-            send_sem=halo_send.at[k, slot],
-            recv_sem=halo_recv.at[k, slot],
+            send_sem=halo_send.at[k, sem],
+            recv_sem=halo_recv.at[k, sem],
             device_id=device(dy, dz),
             device_id_type=MESH,
         )
 
-    def send_halos(slot, fields):
+    def send_halos(slot, low_field, fields, sem):
         for hop in hops:
             if hop[1] == 0:
 
                 @pl.when(exists(*hop))
                 def _():
-                    halo(hop, slot, fields).start()
-
-        for f in range(fields):
+                    halo(hop, slot, low_field, fields, sem).start()
+
+        for f in range(low_field, low_field + fields):
             low = jnp.zeros((own, tz), jnp.float32)
             high = jnp.zeros((own, tz), jnp.float32)
             for x in range(full_x):
@@ -511,22 +524,22 @@
 
                 @pl.when(exists(*hop))
                 def _():
-                    halo(hop, slot, fields).start()
-
-    def take_halos(slot, fields):
+                    halo(hop, slot, low_field, fields, sem).start()
+
+    def take_halos(slot, low_field, fields, sem):
         for hop in hops:
 
             @pl.when(exists(-hop[0], -hop[1]))
             def _():
-                halo(hop, slot, fields).wait_recv()
+                halo(hop, slot, low_field, fields, sem).wait_recv()
 
         for hop in hops:
 
             @pl.when(exists(*hop))
             def _():
-                halo(hop, slot, fields).wait_send()
-
-        for f in range(fields):
+                halo(hop, slot, low_field, fields, sem).wait_send()
+
+        for f in range(low_field, low_field + fields):
             from_low = land_z[slot, 0, f]
             from_high = land_z[slot, 1, f]
             for x in range(full_x):
@@ -543,16 +556,21 @@
 
         @pl.when(distant(i))
         def _():
-            swap(0, i).wait_recv()
-
-    send_halos(0, 3)
+            swap(0, i, 0).wait_recv()
+
+    send_halos(0, 0, 2, 0)
+    for i in range(nx):
+
+        @pl.when(distant(i))
+        def _():
+            swap(0, i, 1).wait_recv()
+
+    send_halos(0, 2, 1, 2)
 
     cells = full_x * rows
-    row = lax.broadcasted_iota(jnp.int32, (cells, tag_ref.shape[1]), 0)
-
-    def receivers(tag, trace):
-        cell = tag[0:1, :]
-        kind = tag[1:2, :]
+    row = lax.broadcasted_iota(jnp.int32, (cells, trace_ref.shape[1]), 0)
+
+    def receivers(cell, kind, trace):
         weight = jnp.zeros(kind.shape, jnp.float32)
         for c in range(table_ref.shape[0]):
             weight = jnp.where(kind == c, table_ref[c], weight)
@@ -576,11 +594,11 @@
 
     @pl.when(on_top)
     def _():
-        total = receivers(tags[0], traces[0])
+        total = receivers(cell_rows[0], class_rows[0], traces[0])
         for d in range(1, nx):
             for c in gather(d):
                 c.wait()
-            total = total + receivers(tags[d], traces[d])
+            total = total + receivers(cell_rows[d], class_rows[d], traces[d])
         for x in range(full_x):
             sources[x, :, 0:steps] = total[x * rows : (x + 1) * rows]
 
@@ -588,7 +606,8 @@
 
         @pl.when(apart(t))
         def _():
-            swap(t, gx).wait_send()
+            swap(t, gx, 0).wait_send()
+            swap(t, gx, 1).wait_send()
 
     wide = 2 * tz
 
@@ -617,13 +636,14 @@
 
         lax.fori_loop(0, DEEP // 2, double_step, 0)
 
-    take_halos(0, 3)
+    take_halos(0, 0, 2, 0)
+    take_halos(0, 2, 1, 2)
     advance(0)
 
     def round_of(r, carry):
         slot = r % 2
-        send_halos(slot, 2)
-        take_halos(slot, 2)
+        send_halos(slot, 0, 2, slot)
+        take_halos(slot, 0, 2, slot)
         advance(r)
         return carry
 
@@ -679,14 +699,15 @@
         pltpu.VMEM((2, 3, own, tz), jnp.float32),
         pltpu.VMEM((full_x, rows, tz), jnp.float32),
         pltpu.VMEM((nx, steps, count), jnp.bfloat16),
-        pltpu.VMEM((nx, 2, count), jnp.int32),
+        pltpu.VMEM((nx, 1, count), jnp.int32),
+        pltpu.VMEM((nx, 1, count), jnp.int32),
         pltpu.VMEM((tx, ty, tz), jnp.float32),
-        sem((8, 2)),
-        sem((8, 2)),
-        sem((nx,)),
-        sem((nx,)),
+        sem((8, 3)),
+        sem((8, 3)),
         sem((nx, 2)),
         sem((nx, 2)),
+        sem((nx, 3)),
+        sem((nx, 3)),
         sem((nx,)),
         sem((nx,)),
         pltpu.VMEM((tx // 2, ty // 2), jnp.int32),
@@ -729,25 +750,26 @@
 def local(counts, traces, receiver_cell, weight_class, weight_table, top, thick, courant, now, before):
     tx, ty, tz = courant.shape
     count, steps = traces.shape
-    tag = jnp.stack([receiver_cell, weight_class])
     vmem = pl.BlockSpec(memory_space=pltpu.VMEM)
     smem = pl.BlockSpec(memory_space=pltpu.SMEM)
     if slabs_fit(counts, tx, ty, tz, steps):
         body, number, place = slab_kernel, 1, pl.BlockSpec(memory_space=pl.ANY)
+        tags = [receiver_cell[None], weight_class[None]]
         scratch = slab_scratch(counts, tx, ty, tz, count, steps)
     else:
         body, number, place = kernel, 0, vmem
+        tags = [jnp.stack([receiver_cell, weight_class])]
         scratch = face_scratch(counts, tx, ty, tz, count, steps)
     return pl.pallas_call(
         functools.partial(body, counts, ty * counts[1], steps),
         out_shape=jax.ShapeDtypeStruct((tx, ty, tz), jnp.float32),
-        in_specs=[place, place, smem, place, place, place, place, place],
+        in_specs=[place] * (1 + len(tags)) + [smem] + [place] * 5,
         out_specs=vmem,
         scratch_shapes=scratch,
         compiler_params=pltpu.CompilerParams(
             collective_id=number, has_side_effects=True, vmem_limit_bytes=56 * 1024 * 1024
         ),
-    )(traces.T, tag, weight_table, top, thick, courant, now, before)
+    )(traces.T, *tags, weight_table, top, thick, courant, now, before)
 
 
 def solution(mesh):

time: 58.6 us -> 57 us (0.973)
  local copies, waits for them, and re-layouts: 2.26 us -> 1.57 us
  other arithmetic: 0.6 us -> 0 us
    unnamed x5 -> x1, local copies, waits for them, and re-layouts: 2.26 us -> 1.57 us
    another operation x1 -> x0, other arithmetic: 0.6 us -> none  [local(): tag = jnp.stack([receiver_cell, weight_class])]
where the time goes in v4:
time: 57 us; the launch traced here: 56.8 us
  Pallas kernels  55.3 us (97%)
  local copies, waits for them, and re-layouts  1.57 us (3%)
    pallas_call x1, Pallas kernels, local(): pl.pallas_call(functools.partial(body, counts, ty * counts[1], steps), ou...  55.3 us
    unnamed x1, local copies, waits for them, and re-layouts  1.57 us

profile of v4, /device:TPU:0, one launch (start us, length us, event | category | flops | bytes accessed | tf_op | source)
XLA Modules:
  0.0 56.8 jit_solution(2979977468010308652)
XLA Ops:
  0.0 55.3 %shard_map.91 = f32[4,64,128]{2,1,0:T(8,128)} custom-call(bf16[32,512]{1,0:T(8,128)(2,1)} %bitcast.3, s32[1,512]{1,0:T(1,128)} %bitcast.4, s32[1,512]{1,0:T(1,128)} %bitcast.5, f32[16]{0:T(128)} %table_ref.1, s32[2,32]{1,0:T(2,128)} %top_ref.1, s32[2,32]{1,0:T(2,128)} %thick_ref.1, f32[4,64,128]{2,1,0:T(8,128)} %courant_ref.1, f32[4,64,128]{2,1,0:T(8,128)} %now_ref.1, ...), custom_call_target="tpu_custom_call" | custom-call | tf_op jit(solution)/shard_map/pallas_call | solution.py:763
  55.3 1.6 %copy.11 = f32[4,64,128]{2,1,0:T(8,128)} copy(f32[4,64,128]{2,1,0:T(8,128)} %shard_map.91) | data formatting | bytes 262144
